TPU v7x, 32 devices: a whole 2x2x4 slice. The times are simulated.
32 devices in a mesh: grp: 2 (over y), dom: 16 (over z, x, core).
Axes of the slice: x: 2, y: 2, z: 4, core: 2. Of those that a mesh axis runs over, the one named last changes fastest.
Arguments:
- atm_state: float32 [2, 16, 512, 2048], P(None, None, ('grp', 'dom')), may hold values from -6 to 6
- ocean_state: float32 [2, 16, 128, 512], P(None, None, 'dom', 'grp'), may hold values from -6 to 6
- atm_levels: float32 [16, 16], replicated, may hold values from -1.5 to 1.5
- ocean_levels: float32 [16, 16], replicated, may hold values from -1.5 to 1.5
- tile_weight: bfloat16 [8192, 128, 128], P(('grp', 'dom')), may hold values from 0 to 0.049804688
- tile_owner: int32 [8192, 1], P(('grp', 'dom')), may hold values from 0 to 31; in each aligned block of 256 rows (0 to 255, 256 to 511, ...) at most 12 rows name the same one
- tile_block: int32 [8192], P(('grp', 'dom')), may hold values from 0 to 15
- tile_source: int32 [8192], P(('grp', 'dom')), may hold values from 0 to 255
- tile_count: int32 [32], P(('grp', 'dom')), may hold values from 128 to 256, as said below
Outputs:
- atm_final: float32 [2, 16, 512, 2048], P(None, None, ('grp', 'dom'))
- ocean_final: float32 [2, 16, 128, 512], P(None, None, 'dom', 'grp')
Inputs may be any that keep to these rules, and one draw needn't show every extreme that they name: `tile_owner`: among the 256 entries of one device's list, at most 12 name the same ocean device, live or not. `tile_count`: entries of a device's list at or past its count are padding and are ignored; some device's count is 256.
All inputs are finite; a program needn't handle non-finite values.
Results may differ from a plain program's by a relative error of at most 0.002.
Values may be sent and summed in bfloat16 or wider, within the bound.
A program may use at most 128 MiB of HBM per device.

v0:
```python
import jax
import jax.numpy as jnp
from jax import lax
from jax.sharding import PartitionSpec as P

STEPS = 4


diffuse = 0.2
vertical = 0.25
couple = 0.5


def padded_2(block, sides, width, periodic):
    for axis, dim in sides:
        count = lax.axis_size(axis)
        forward = [(i, i + 1) for i in range(count - 1)]
        if periodic:
            forward.append((count - 1, 0))
        backward = [(target, source) for source, target in forward]
        low = lax.ppermute(
            lax.slice_in_dim(block, block.shape[dim] - width, None, axis=dim), axis, forward
        )
        high = lax.ppermute(lax.slice_in_dim(block, 0, width, axis=dim), axis, backward)
        block = jnp.concatenate([low, block, high], axis=dim)
    return block


def atmos_core(extended, levels):
    center = extended[:, :, 1:-1]
    along_x = extended[:, :, 2:] + extended[:, :, :-2]
    padded = jnp.pad(center, ((0, 0), (0, 0), (0, 0), (1, 1)))
    along_y = padded[..., 2:] + padded[..., :-2]
    mixing = jnp.einsum("lm,vmxy->vlxy", levels, center, precision=lax.Precision.HIGHEST)
    return center + diffuse * (along_x + along_y - 4.0 * center) + vertical * mixing


def ocean_core(extended, levels):
    center = extended[:, :, 1:-1, 1:-1]
    along_x = extended[:, :, 2:, 1:-1] + extended[:, :, :-2, 1:-1]
    along_y = extended[:, :, 1:-1, 2:] + extended[:, :, 1:-1, :-2]
    mixing = jnp.einsum("lm,vmxy->vlxy", levels, center, precision=lax.Precision.HIGHEST)
    return center + diffuse * (along_x + along_y - 4.0 * center) + vertical * mixing


def per_device(
    atm_state,
    ocean_state,
    atm_levels,
    ocean_levels,
    tile_weight,
    tile_owner,
    tile_block,
    tile_source,
    tile_count,
):
    devices = lax.axis_size(("grp", "dom"))
    tiles = tile_weight.shape[0]
    capacity = max(2, 3 * tiles // (2 * devices))
    variables = atm_state.shape[0]
    ocean_blocks = ocean_state.shape[2] * ocean_state.shape[3] // 128
    atmos_blocks = atm_state.shape[2] * atm_state.shape[3] // 128
    live_rows = jnp.arange(tiles, dtype=jnp.int32) < tile_count[0]
    target = tile_owner[:, 0]
    surface = (
        atm_state[:, 0]
        .astype(jnp.bfloat16)
        .reshape(variables, atmos_blocks, 128)
        .transpose(1, 0, 2)
    )
    picked = surface[tile_source]
    contrib = jnp.einsum("tfa,tao->tfo", picked, tile_weight, preferred_element_type=jnp.float32)
    contrib = jnp.where(live_rows[:, None, None], contrib, 0.0)
    ocean_surface = ocean_state[:, 0].reshape(variables, ocean_blocks, 128).transpose(1, 0, 2)
    onehot = (target[:, None] == jnp.arange(devices, dtype=jnp.int32)[None, :]).astype(jnp.int32)
    onehot = onehot * live_rows[:, None].astype(jnp.int32)
    order_rank = jnp.cumsum(onehot, axis=0) - onehot
    tile_rank = jnp.take_along_axis(order_rank, target[:, None], axis=1)[:, 0]
    slot_index = jnp.where(live_rows, target * capacity + tile_rank, devices * capacity)
    outbox = (
        jnp.zeros((devices * capacity, variables, 128), jnp.float32)
        .at[slot_index]
        .set(contrib, mode="drop")
    )
    slot_block = (
        jnp.full((devices * capacity,), -1, jnp.int32).at[slot_index].set(tile_block, mode="drop")
    )
    inbox, inbox_block = (
        lax.all_to_all(outbox, ("grp", "dom"), split_axis=0, concat_axis=0, tiled=True),
        lax.all_to_all(slot_block, ("grp", "dom"), split_axis=0, concat_axis=0, tiled=True),
    )
    selector = (jnp.arange(ocean_blocks, dtype=jnp.int32)[:, None] == inbox_block[None, :]).astype(
        jnp.float32
    )
    received = jnp.dot(
        selector,
        inbox.reshape(devices * capacity, variables * 128),
        precision=lax.Precision.HIGHEST,
    )
    received = received.reshape(ocean_blocks, variables, 128)
    flux = received - ocean_surface
    flux_sent = flux.astype(jnp.bfloat16)
    outgoing = flux_sent[jnp.maximum(inbox_block, 0)]
    returned_slots = lax.all_to_all(
        outgoing, ("grp", "dom"), split_axis=0, concat_axis=0, tiled=True
    )
    flux_tiles = returned_slots[jnp.minimum(slot_index, devices * capacity - 1)]
    back_terms = jnp.einsum(
        "tfo,tao->tfa", flux_tiles, tile_weight, preferred_element_type=jnp.float32
    )
    back_terms = jnp.where(live_rows[:, None, None], back_terms, 0.0)
    to_block = (jnp.arange(atmos_blocks, dtype=jnp.int32)[:, None] == tile_source[None, :]).astype(
        jnp.float32
    )
    returned = jnp.dot(
        to_block, back_terms.reshape(tiles, variables * 128), precision=lax.Precision.HIGHEST
    )
    returned_field = (
        returned.reshape(atmos_blocks, variables, 128)
        .transpose(1, 0, 2)
        .reshape(variables, atm_state.shape[2], atm_state.shape[3])
    )
    flux_field = flux.transpose(1, 0, 2).reshape(
        variables, ocean_state.shape[2], ocean_state.shape[3]
    )
    atmos = atm_state
    for repeat in range(STEPS):
        extended = padded_2(atmos, ((("grp", "dom"), 2),), 1, True)
        atmos = atmos_core(extended, atm_levels)
    ocean = ocean_state
    for repeat in range(STEPS):
        extended = padded_2(ocean, (("grp", 3), ("dom", 2)), 1, False)
        ocean = ocean_core(extended, ocean_levels)
    atm_final = atmos.at[:, 0].add(-couple * returned_field)
    ocean_final = ocean.at[:, 0].add(couple * flux_field)
    return (atm_final, ocean_final)


def solution(mesh):
    in_specs = (
        P(None, None, ("grp", "dom"), None),
        P(None, None, "dom", "grp"),
        P(),
        P(),
        P(("grp", "dom"), None, None),
        P(("grp", "dom"), None),
        P(("grp", "dom")),
        P(("grp", "dom")),
        P(("grp", "dom")),
    )
    out_specs = (P(None, None, ("grp", "dom"), None), P(None, None, "dom", "grp"))
    return jax.shard_map(
        per_device, mesh=mesh, in_specs=in_specs, out_specs=out_specs, check_vma=False
    )
```

profile of v0, /device:TPU:0, one launch (start us, length us, event | category | flops | bytes accessed | tf_op | source)
XLA Modules:
  0.0 219.9 jit_solution(13925229761317796292)
XLA Ops:
  0.7 4.7 %copy.85 = f32[2,16,16,2048]{3,1,2,0:T(8,128)S(1)} copy(f32[2,16,16,2048]{3,2,1,0:T(8,128)} %param.13) | data formatting | bytes 8388608 | tf_op args[0]
  7.9 6.0 %collective-permute-start = (f32[2,16,1,2048]{3,1,2,0:T(8,128)S(1)}, f32[2,16,1,2048]{3,1,2,0:T(8,128)S(1)}, u32[]{:S(2)}, u32[]{:S(2)}) collective-permute-start(f32[2,16,1,2048]{3,1,2,0:T(8,128)S(1)} %get-tuple-element.44), channel_id=1, source_target_pairs={{1,0},{2,1},{3,2},{4,3},{5,4},{6,5},{7,6},{8,7},{9,8},{10,9},{11,1... | collective-permute-start | bytes 786440 | tf_op jit(solution)/shard_map/ppermute | solution.py:24
  14.1 3.8 %collective-permute-start.8 = (f32[2,16,8,1]{3,1,2,0:T(8,128)S(1)}, f32[2,16,8,1]{3,1,2,0:T(8,128)S(1)}, u32[]{:S(2)}, u32[]{:S(2)}) collective-permute-start(f32[2,16,8,1]{3,1,2,0:T(8,128)S(1)} %get-tuple-element.61), channel_id=1, source_target_pairs={{0,16},{1,17},{2,18},{3,19},{4,20},{5,21},{6,22},{7,23},{8,24},{9,... | collective-permute-start | bytes 3080 | tf_op jit(solution)/shard_map/ppermute | solution.py:21
  25.5 3.4 %all-to-all-start = ((s32[32,12,1]{1,2,0:T(1,128)}), s32[32,12,1]{1,2,0:T(1,128)S(1)}, u32[]{:S(2)}, u32[]{:S(2)}) async-start(s32[32,12,1]{1,2,0:T(1,128)} %bitcast.17), calls=%async_computation | async-start | bytes 32768 | tf_op jit(solution)/shard_map/all_to_all | solution.py:90
  35.9 3.4 %collective-permute-start.12 = (f32[2,16,8,1]{3,1,2,0:T(8,128)S(1)}, f32[2,16,8,1]{3,1,2,0:T(8,128)S(1)}, u32[]{:S(2)}, u32[]{:S(2)}) collective-permute-start(f32[2,16,8,1]{3,1,2,0:T(8,128)S(1)} %get-tuple-element.59), channel_id=1, source_target_pairs={{0,16},{1,17},{2,18},{3,19},{4,20},{5,21},{6,22},{7,23},{8,24},{9,... | collective-permute-start | bytes 3080 | tf_op jit(solution)/shard_map/ppermute | solution.py:21
  42.8 3.4 %collective-permute-done.13 = f32[2,16,8,1]{3,1,2,0:T(8,128)S(1)} collective-permute-done((f32[2,16,8,1]{3,1,2,0:T(8,128)S(1)}, f32[2,16,8,1]{3,1,2,0:T(8,128)S(1)}, u32[]{:S(2)}, u32[]{:S(2)}) %collective-permute-start.13) | collective-permute-done | bytes 1056 | tf_op jit(solution)/shard_map/ppermute | solution.py:24
  46.3 3.3 %collective-permute-start.15 = (f32[2,16,1,258]{3,1,2,0:T(8,128)S(1)}, f32[2,16,1,258]{3,1,2,0:T(8,128)S(1)}, u32[]{:S(2)}, u32[]{:S(2)}) collective-permute-start(f32[2,16,1,258]{3,1,2,0:T(8,128)S(1)} %get-tuple-element.51), channel_id=1, source_target_pairs={{0,1},{1,2},{2,3},{3,4},{4,5},{5,6},{6,7},{7,8},{8,9},{9,10},{10,1... | collective-permute-start | bytes 99080 | tf_op jit(solution)/shard_map/ppermute | solution.py:21
  50.9 5.7 %convolution_select_fusion.1 = f32[256,2,128]{2,1,0:T(2,128)S(1)} fusion(bf16[256,2,128]{2,1,0:T(2,128)(2,1)S(1)} %gather_fusion, bf16[256,128,128]{2,1,0:T(8,128)(2,1)} %param.17, pred[256]{0:T(512)(128)(4,1)S(1)} %get-tuple-element.64), kind=kOutput, calls=%fused_computation.64 | convolution fusion | flops 16842752 | bytes 8782080 | tf_op jit(solution)/shard_map/tfa,tao->tfo/dot_general | solution.py:72
  61.3 24.1 %scatter_fusion = f32[384,2,128]{2,1,0:T(2,128)} fusion(f32[384,2,128]{2,1,0:T(2,128)} %broadcast_in_dim.49, s32[256]{0:T(256)S(1)} %bitcast.140, f32[256,2,128]{2,1,0:T(2,128)S(1)} %convolution_select_fusion.1), kind=kCustom, calls=%fused_computation.5 | custom fusion | bytes 787456 | tf_op jit(solution)/shard_map/scatter | solution.py:83
  85.5 3.1 %collective-permute-start.19 = (f32[2,16,1,258]{3,1,2,0:T(8,128)S(1)}, f32[2,16,1,258]{3,1,2,0:T(8,128)S(1)}, u32[]{:S(2)}, u32[]{:S(2)}) collective-permute-start(f32[2,16,1,258]{3,1,2,0:T(8,128)S(1)} %get-tuple-element.49), channel_id=1, source_target_pairs={{0,1},{1,2},{2,3},{3,4},{4,5},{5,6},{6,7},{7,8},{8,9},{9,10},{10,1... | collective-permute-start | bytes 99080 | tf_op jit(solution)/shard_map/ppermute | solution.py:21
  90.0 12.2 %all-to-all-start.1 = ((f32[384,2,128]{2,1,0:T(2,128)}), f32[384,2,128]{2,1,0:T(2,128)S(1)}, u32[]{:S(2)}, u32[]{:S(2)}) async-start(f32[384,2,128]{2,1,0:T(2,128)} %scatter_fusion), calls=%async_computation.1 | async-start | bytes 786432 | tf_op jit(solution)/shard_map/all_to_all | solution.py:89
  104.0 12.7 %fusion.5 = f32[2,16,16,2048]{3,1,2,0:T(8,128)S(1)} fusion(f32[2,16,16,2048]{3,1,2,0:T(8,128)} %copy-done.1, f32[2,16,1,2048]{3,1,2,0:T(8,128)S(1)} %collective-permute-done.1, f32[2,16,1,2048]{3,1,2,0:T(8,128)S(1)} %collective-permute-done, f32[16,16]{1,0:T(8,128)S(1)} %copy-done), kind=kOutput, calls=%fused_computation.19 | convolution fusion | flops 212860928 | bytes 13108224 | tf_op jit(solution)/shard_map/lm,vmxy->vlxy/dot_general | solution.py:34
  116.9 5.3 %collective-permute-start.2 = (f32[2,16,1,2048]{3,1,2,0:T(8,128)S(1)}, f32[2,16,1,2048]{3,1,2,0:T(8,128)S(1)}, u32[]{:S(2)}, u32[]{:S(2)}) collective-permute-start(f32[2,16,1,2048]{3,1,2,0:T(8,128)S(1)} %get-tuple-element.42), channel_id=1, source_target_pairs={{1,0},{2,1},{3,2},{4,3},{5,4},{6,5},{7,6},{8,7},{9,8},{10,9},{11,1... | collective-permute-start | bytes 786440 | tf_op jit(solution)/shard_map/ppermute | solution.py:24
  122.3 3.5 %collective-permute-start.20 = (f32[2,16,8,1]{3,1,2,0:T(8,128)S(1)}, f32[2,16,8,1]{3,1,2,0:T(8,128)S(1)}, u32[]{:S(2)}, u32[]{:S(2)}) collective-permute-start(f32[2,16,8,1]{3,1,2,0:T(8,128)S(1)} %get-tuple-element.55), channel_id=1, source_target_pairs={{0,16},{1,17},{2,18},{3,19},{4,20},{5,21},{6,22},{7,23},{8,24},{9,... | collective-permute-start | bytes 3080 | tf_op jit(solution)/shard_map/ppermute | solution.py:21
  128.3 4.4 %collective-permute-done.21 = f32[2,16,8,1]{3,1,2,0:T(8,128)S(1)} collective-permute-done((f32[2,16,8,1]{3,1,2,0:T(8,128)S(1)}, f32[2,16,8,1]{3,1,2,0:T(8,128)S(1)}, u32[]{:S(2)}, u32[]{:S(2)}) %collective-permute-start.21) | collective-permute-done | bytes 1056 | tf_op jit(solution)/shard_map/ppermute | solution.py:24
  135.4 12.7 %fusion.11 = f32[2,16,16,2048]{3,1,2,0:T(8,128)S(1)} fusion(f32[2,16,16,2048]{3,1,2,0:T(8,128)} %copy-done.3, f32[2,16,1,2048]{3,1,2,0:T(8,128)S(1)} %collective-permute-done.3, f32[2,16,1,2048]{3,1,2,0:T(8,128)S(1)} %collective-permute-done.2, f32[16,16]{1,0:T(8,128)S(1)} %copy-done), kind=kOutput, calls=%fused_computation.25 | convolution fusion | flops 212860928 | bytes 13108224 | tf_op jit(solution)/shard_map/lm,vmxy->vlxy/dot_general | solution.py:34
  149.4 4.2 %collective-permute-start.4 = (f32[2,16,1,2048]{3,1,2,0:T(8,128)S(1)}, f32[2,16,1,2048]{3,1,2,0:T(8,128)S(1)}, u32[]{:S(2)}, u32[]{:S(2)}) collective-permute-start(f32[2,16,1,2048]{3,1,2,0:T(8,128)S(1)} %get-tuple-element.40), channel_id=1, source_target_pairs={{1,0},{2,1},{3,2},{4,3},{5,4},{6,5},{7,6},{8,7},{9,8},{10,9},{11,1... | collective-permute-start | bytes 786440 | tf_op jit(solution)/shard_map/ppermute | solution.py:24
  159.7 12.7 %fusion.17 = f32[2,16,16,2048]{3,1,2,0:T(8,128)S(1)} fusion(f32[2,16,16,2048]{3,1,2,0:T(8,128)} %copy-done.4, f32[2,16,1,2048]{3,1,2,0:T(8,128)S(1)} %collective-permute-done.5, f32[2,16,1,2048]{3,1,2,0:T(8,128)S(1)} %collective-permute-done.4, f32[16,16]{1,0:T(8,128)S(1)} %copy-done), kind=kOutput, calls=%fused_computation.31 | convolution fusion | flops 212860928 | bytes 13108224 | tf_op jit(solution)/shard_map/lm,vmxy->vlxy/dot_general | solution.py:34
  172.6 5.3 %collective-permute-start.6 = (f32[2,16,1,2048]{3,1,2,0:T(8,128)S(1)}, f32[2,16,1,2048]{3,1,2,0:T(8,128)S(1)}, u32[]{:S(2)}, u32[]{:S(2)}) collective-permute-start(f32[2,16,1,2048]{3,1,2,0:T(8,128)S(1)} %get-tuple-element.38), channel_id=1, source_target_pairs={{1,0},{2,1},{3,2},{4,3},{5,4},{6,5},{7,6},{8,7},{9,8},{10,9},{11,1... | collective-permute-start | bytes 786440 | tf_op jit(solution)/shard_map/ppermute | solution.py:24
  178.9 3.2 %collective-permute-done.7 = f32[2,16,1,2048]{3,1,2,0:T(8,128)S(1)} collective-permute-done((f32[2,16,1,2048]{3,1,2,0:T(8,128)S(1)}, f32[2,16,1,2048]{3,1,2,0:T(8,128)S(1)}, u32[]{:S(2)}, u32[]{:S(2)}) %collective-permute-start.7) | collective-permute-done | bytes 262176 | tf_op jit(solution)/shard_map/ppermute | solution.py:21
  182.1 14.1 %fusion.23 = f32[2,16,16,2048]{3,1,2,0:T(8,128)} fusion(f32[2,16,16,2048]{3,1,2,0:T(8,128)} %copy-done.5, f32[2,16,1,2048]{3,1,2,0:T(8,128)S(1)} %collective-permute-done.7, f32[2,16,1,2048]{3,1,2,0:T(8,128)S(1)} %collective-permute-done.6, f32[16,16]{1,0:T(8,128)S(1)} %copy-done), kind=kOutput, calls=%fused_computation.37 | convolution fusion | flops 212860928 | bytes 13108224 | tf_op jit(solution)/shard_map/lm,vmxy->vlxy/dot_general | solution.py:34
  197.1 7.8 %convolution_select_fusion = f32[256,2,128]{2,1,0:T(2,128)S(1)} fusion(bf16[256,2,128]{2,1,0:T(2,128)(2,1)S(1)} %gather_fusion.2, bf16[256,128,128]{2,1,0:T(8,128)(2,1)} %param.17, pred[256]{0:T(512)(128)(4,1)S(1)} %get-tuple-element.64), kind=kOutput, calls=%fused_computation.63 | convolution fusion | flops 16842752 | bytes 8782080 | tf_op jit(solution)/shard_map/tfo,tao->tfa/dot_general | solution.py:108
  207.3 6.0 %scatter-add.6 = f32[2,16,16,2048]{3,1,2,0:T(8,128)} dynamic-update-slice(f32[2,16,16,2048]{3,1,2,0:T(8,128)} %fusion.23, f32[2,1,16,2048]{3,1,2,0:T(1,128)S(1)} %slice_add_fusion, s32[]{:T(128)} %constant.91.clone.1, s32[]{:T(128)} %constant.91.clone.1, s32[]{:T(128)} %constant.91.clone.1, s32[]{:T(128)} %constant.91.clone.1) | dynamic-update-slice | bytes 524292 | tf_op jit(solution)/shard_map/scatter-add | solution.py:134
  213.3 6.6 %copy.102 = f32[2,16,16,2048]{3,2,1,0:T(8,128)} copy(f32[2,16,16,2048]{3,1,2,0:T(8,128)} %scatter-add.6) | data formatting | bytes 8388608
  (121 shorter events, 46.4 us)
Async XLA Ops:
  7.4 96.6 %collective-permute-start.1 = (f32[2,16,1,2048]{3,1,2,0:T(8,128)S(1)}, f32[2,16,1,2048]{3,1,2,0:T(8,128)S(1)}, u32[]{:S(2)}, u32[]{:S(2)}) collective-permute-start(f32[2,16,1,2048]{3,1,2,0:T(8,128)S(1)} %get-tuple-element.45), channel_id=1, source_target_pairs={{0,1},{1,2},{2,3},{3,4},{4,5},{5,6},{6,7},{7,8},{8,9},{9,10},{10,1... | collective-permute-start | bytes 786440 | tf_op jit(solution)/shard_map/ppermute | solution.py:21
  7.9 96.1 %collective-permute-start = (f32[2,16,1,2048]{3,1,2,0:T(8,128)S(1)}, f32[2,16,1,2048]{3,1,2,0:T(8,128)S(1)}, u32[]{:S(2)}, u32[]{:S(2)}) collective-permute-start(f32[2,16,1,2048]{3,1,2,0:T(8,128)S(1)} %get-tuple-element.44), channel_id=1, source_target_pairs={{1,0},{2,1},{3,2},{4,3},{5,4},{6,5},{7,6},{8,7},{9,8},{10,9},{11,1... | collective-permute-start | bytes 786440 | tf_op jit(solution)/shard_map/ppermute | solution.py:24
  14.1 14.8 %collective-permute-start.8 = (f32[2,16,8,1]{3,1,2,0:T(8,128)S(1)}, f32[2,16,8,1]{3,1,2,0:T(8,128)S(1)}, u32[]{:S(2)}, u32[]{:S(2)}) collective-permute-start(f32[2,16,8,1]{3,1,2,0:T(8,128)S(1)} %get-tuple-element.61), channel_id=1, source_target_pairs={{0,16},{1,17},{2,18},{3,19},{4,20},{5,21},{6,22},{7,23},{8,24},{9,... | collective-permute-start | bytes 3080 | tf_op jit(solution)/shard_map/ppermute | solution.py:21
  17.9 11.0 %collective-permute-start.9 = (f32[2,16,8,1]{3,1,2,0:T(8,128)S(1)}, f32[2,16,8,1]{3,1,2,0:T(8,128)S(1)}, u32[]{:S(2)}, u32[]{:S(2)}) collective-permute-start(f32[2,16,8,1]{3,1,2,0:T(8,128)S(1)} %get-tuple-element.60), channel_id=1, source_target_pairs={{16,0},{17,1},{18,2},{19,3},{20,4},{21,5},{22,6},{23,7},{24,8},{25... | collective-permute-start | bytes 3080 | tf_op jit(solution)/shard_map/ppermute | solution.py:24
  25.5 64.5 %all-to-all-start = ((s32[32,12,1]{1,2,0:T(1,128)}), s32[32,12,1]{1,2,0:T(1,128)S(1)}, u32[]{:S(2)}, u32[]{:S(2)}) async-start(s32[32,12,1]{1,2,0:T(1,128)} %bitcast.17), calls=%async_computation | async-start | bytes 32768 | tf_op jit(solution)/shard_map/all_to_all | solution.py:90
  35.9 6.8 %collective-permute-start.12 = (f32[2,16,8,1]{3,1,2,0:T(8,128)S(1)}, f32[2,16,8,1]{3,1,2,0:T(8,128)S(1)}, u32[]{:S(2)}, u32[]{:S(2)}) collective-permute-start(f32[2,16,8,1]{3,1,2,0:T(8,128)S(1)} %get-tuple-element.59), channel_id=1, source_target_pairs={{0,16},{1,17},{2,18},{3,19},{4,20},{5,21},{6,22},{7,23},{8,24},{9,... | collective-permute-start | bytes 3080 | tf_op jit(solution)/shard_map/ppermute | solution.py:21
  39.3 6.9 %collective-permute-start.13 = (f32[2,16,8,1]{3,1,2,0:T(8,128)S(1)}, f32[2,16,8,1]{3,1,2,0:T(8,128)S(1)}, u32[]{:S(2)}, u32[]{:S(2)}) collective-permute-start(f32[2,16,8,1]{3,1,2,0:T(8,128)S(1)} %get-tuple-element.58), channel_id=1, source_target_pairs={{16,0},{17,1},{18,2},{19,3},{20,4},{21,5},{22,6},{23,7},{24,8},{25... | collective-permute-start | bytes 3080 | tf_op jit(solution)/shard_map/ppermute | solution.py:24
  46.3 10.2 %collective-permute-start.15 = (f32[2,16,1,258]{3,1,2,0:T(8,128)S(1)}, f32[2,16,1,258]{3,1,2,0:T(8,128)S(1)}, u32[]{:S(2)}, u32[]{:S(2)}) collective-permute-start(f32[2,16,1,258]{3,1,2,0:T(8,128)S(1)} %get-tuple-element.51), channel_id=1, source_target_pairs={{0,1},{1,2},{2,3},{3,4},{4,5},{5,6},{6,7},{7,8},{8,9},{9,10},{10,1... | collective-permute-start | bytes 99080 | tf_op jit(solution)/shard_map/ppermute | solution.py:21
  49.6 7.0 %collective-permute-start.14 = (f32[2,16,1,258]{3,1,2,0:T(8,128)S(1)}, f32[2,16,1,258]{3,1,2,0:T(8,128)S(1)}, u32[]{:S(2)}, u32[]{:S(2)}) collective-permute-start(f32[2,16,1,258]{3,1,2,0:T(8,128)S(1)} %get-tuple-element.50), channel_id=1, source_target_pairs={{1,0},{2,1},{3,2},{4,3},{5,4},{6,5},{7,6},{8,7},{9,8},{10,9},{11,1... | collective-permute-start | bytes 99080 | tf_op jit(solution)/shard_map/ppermute | solution.py:24
  57.1 28.4 %collective-permute-start.16 = (f32[2,16,8,1]{3,1,2,0:T(8,128)S(1)}, f32[2,16,8,1]{3,1,2,0:T(8,128)S(1)}, u32[]{:S(2)}, u32[]{:S(2)}) collective-permute-start(f32[2,16,8,1]{3,1,2,0:T(8,128)S(1)} %get-tuple-element.57), channel_id=1, source_target_pairs={{0,16},{1,17},{2,18},{3,19},{4,20},{5,21},{6,22},{7,23},{8,24},{9,... | collective-permute-start | bytes 3080 | tf_op jit(solution)/shard_map/ppermute | solution.py:21
  59.1 26.3 %collective-permute-start.17 = (f32[2,16,8,1]{3,1,2,0:T(8,128)S(1)}, f32[2,16,8,1]{3,1,2,0:T(8,128)S(1)}, u32[]{:S(2)}, u32[]{:S(2)}) collective-permute-start(f32[2,16,8,1]{3,1,2,0:T(8,128)S(1)} %get-tuple-element.56), channel_id=1, source_target_pairs={{16,0},{17,1},{18,2},{19,3},{20,4},{21,5},{22,6},{23,7},{24,8},{25... | collective-permute-start | bytes 3080 | tf_op jit(solution)/shard_map/ppermute | solution.py:24
  85.5 18.0 %collective-permute-start.19 = (f32[2,16,1,258]{3,1,2,0:T(8,128)S(1)}, f32[2,16,1,258]{3,1,2,0:T(8,128)S(1)}, u32[]{:S(2)}, u32[]{:S(2)}) collective-permute-start(f32[2,16,1,258]{3,1,2,0:T(8,128)S(1)} %get-tuple-element.49), channel_id=1, source_target_pairs={{0,1},{1,2},{2,3},{3,4},{4,5},{5,6},{6,7},{7,8},{8,9},{9,10},{10,1... | collective-permute-start | bytes 99080 | tf_op jit(solution)/shard_map/ppermute | solution.py:21
  88.7 14.9 %collective-permute-start.18 = (f32[2,16,1,258]{3,1,2,0:T(8,128)S(1)}, f32[2,16,1,258]{3,1,2,0:T(8,128)S(1)}, u32[]{:S(2)}, u32[]{:S(2)}) collective-permute-start(f32[2,16,1,258]{3,1,2,0:T(8,128)S(1)} %get-tuple-element.48), channel_id=1, source_target_pairs={{1,0},{2,1},{3,2},{4,3},{5,4},{6,5},{7,6},{8,7},{9,8},{10,9},{11,1... | collective-permute-start | bytes 99080 | tf_op jit(solution)/shard_map/ppermute | solution.py:24
  90.0 64.0 %all-to-all-start.1 = ((f32[384,2,128]{2,1,0:T(2,128)}), f32[384,2,128]{2,1,0:T(2,128)S(1)}, u32[]{:S(2)}, u32[]{:S(2)}) async-start(f32[384,2,128]{2,1,0:T(2,128)} %scatter_fusion), calls=%async_computation.1 | async-start | bytes 786432 | tf_op jit(solution)/shard_map/all_to_all | solution.py:89
  116.8 18.6 %collective-permute-start.3 = (f32[2,16,1,2048]{3,1,2,0:T(8,128)S(1)}, f32[2,16,1,2048]{3,1,2,0:T(8,128)S(1)}, u32[]{:S(2)}, u32[]{:S(2)}) collective-permute-start(f32[2,16,1,2048]{3,1,2,0:T(8,128)S(1)} %get-tuple-element.43), channel_id=1, source_target_pairs={{0,1},{1,2},{2,3},{3,4},{4,5},{5,6},{6,7},{7,8},{8,9},{9,10},{10,1... | collective-permute-start | bytes 786440 | tf_op jit(solution)/shard_map/ppermute | solution.py:21
  116.9 18.5 %collective-permute-start.2 = (f32[2,16,1,2048]{3,1,2,0:T(8,128)S(1)}, f32[2,16,1,2048]{3,1,2,0:T(8,128)S(1)}, u32[]{:S(2)}, u32[]{:S(2)}) collective-permute-start(f32[2,16,1,2048]{3,1,2,0:T(8,128)S(1)} %get-tuple-element.42), channel_id=1, source_target_pairs={{1,0},{2,1},{3,2},{4,3},{5,4},{6,5},{7,6},{8,7},{9,8},{10,9},{11,1... | collective-permute-start | bytes 786440 | tf_op jit(solution)/shard_map/ppermute | solution.py:24
  125.8 6.9 %collective-permute-start.21 = (f32[2,16,8,1]{3,1,2,0:T(8,128)S(1)}, f32[2,16,8,1]{3,1,2,0:T(8,128)S(1)}, u32[]{:S(2)}, u32[]{:S(2)}) collective-permute-start(f32[2,16,8,1]{3,1,2,0:T(8,128)S(1)} %get-tuple-element.54), channel_id=1, source_target_pairs={{16,0},{17,1},{18,2},{19,3},{20,4},{21,5},{22,6},{23,7},{24,8},{25... | collective-permute-start | bytes 3080 | tf_op jit(solution)/shard_map/ppermute | solution.py:24
  132.8 20.8 %collective-permute-start.23 = (f32[2,16,1,258]{3,1,2,0:T(8,128)S(1)}, f32[2,16,1,258]{3,1,2,0:T(8,128)S(1)}, u32[]{:S(2)}, u32[]{:S(2)}) collective-permute-start(f32[2,16,1,258]{3,1,2,0:T(8,128)S(1)} %get-tuple-element.47), channel_id=1, source_target_pairs={{0,1},{1,2},{2,3},{3,4},{4,5},{5,6},{6,7},{7,8},{8,9},{9,10},{10,1... | collective-permute-start | bytes 99080 | tf_op jit(solution)/shard_map/ppermute | solution.py:21
  134.1 19.5 %collective-permute-start.22 = (f32[2,16,1,258]{3,1,2,0:T(8,128)S(1)}, f32[2,16,1,258]{3,1,2,0:T(8,128)S(1)}, u32[]{:S(2)}, u32[]{:S(2)}) collective-permute-start(f32[2,16,1,258]{3,1,2,0:T(8,128)S(1)} %get-tuple-element.46), channel_id=1, source_target_pairs={{1,0},{2,1},{3,2},{4,3},{5,4},{6,5},{7,6},{8,7},{9,8},{10,9},{11,1... | collective-permute-start | bytes 99080 | tf_op jit(solution)/shard_map/ppermute | solution.py:24
  148.2 11.5 %collective-permute-start.5 = (f32[2,16,1,2048]{3,1,2,0:T(8,128)S(1)}, f32[2,16,1,2048]{3,1,2,0:T(8,128)S(1)}, u32[]{:S(2)}, u32[]{:S(2)}) collective-permute-start(f32[2,16,1,2048]{3,1,2,0:T(8,128)S(1)} %get-tuple-element.41), channel_id=1, source_target_pairs={{0,1},{1,2},{2,3},{3,4},{4,5},{5,6},{6,7},{7,8},{8,9},{9,10},{10,1... | collective-permute-start | bytes 786440 | tf_op jit(solution)/shard_map/ppermute | solution.py:21
  149.4 10.3 %collective-permute-start.4 = (f32[2,16,1,2048]{3,1,2,0:T(8,128)S(1)}, f32[2,16,1,2048]{3,1,2,0:T(8,128)S(1)}, u32[]{:S(2)}, u32[]{:S(2)}) collective-permute-start(f32[2,16,1,2048]{3,1,2,0:T(8,128)S(1)} %get-tuple-element.40), channel_id=1, source_target_pairs={{1,0},{2,1},{3,2},{4,3},{5,4},{6,5},{7,6},{8,7},{9,8},{10,9},{11,1... | collective-permute-start | bytes 786440 | tf_op jit(solution)/shard_map/ppermute | solution.py:24
  156.9 39.3 %all-to-all-start.2 = ((bf16[384,2,128]{2,1,0:T(2,128)(2,1)}), bf16[384,2,128]{2,1,0:T(2,128)(2,1)S(1)}, u32[]{:S(2)}, u32[]{:S(2)}) async-start(bf16[384,2,128]{2,1,0:T(2,128)(2,1)} %gather_fusion.1), calls=%async_computation.2 | async-start | bytes 393216 | tf_op jit(solution)/shard_map/all_to_all | solution.py:104
  172.5 9.6 %collective-permute-start.7 = (f32[2,16,1,2048]{3,1,2,0:T(8,128)S(1)}, f32[2,16,1,2048]{3,1,2,0:T(8,128)S(1)}, u32[]{:S(2)}, u32[]{:S(2)}) collective-permute-start(f32[2,16,1,2048]{3,1,2,0:T(8,128)S(1)} %get-tuple-element.39), channel_id=1, source_target_pairs={{0,1},{1,2},{2,3},{3,4},{4,5},{5,6},{6,7},{7,8},{8,9},{9,10},{10,1... | collective-permute-start | bytes 786440 | tf_op jit(solution)/shard_map/ppermute | solution.py:21
  172.6 9.5 %collective-permute-start.6 = (f32[2,16,1,2048]{3,1,2,0:T(8,128)S(1)}, f32[2,16,1,2048]{3,1,2,0:T(8,128)S(1)}, u32[]{:S(2)}, u32[]{:S(2)}) collective-permute-start(f32[2,16,1,2048]{3,1,2,0:T(8,128)S(1)} %get-tuple-element.38), channel_id=1, source_target_pairs={{1,0},{2,1},{3,2},{4,3},{5,4},{6,5},{7,6},{8,7},{9,8},{10,9},{11,1... | collective-permute-start | bytes 786440 | tf_op jit(solution)/shard_map/ppermute | solution.py:24
  (13 other events, 235.6 us)
where the time goes:
time: 221 us; the launch traced here: 220 us
  starting transfers between devices  73.9 us (33%)
  matrix products  68 us (31%)
  local copies, waits for them, and re-layouts  57.2 us (26%)
  waiting for transfers between devices  15 us (7%)
  other arithmetic  3.81 us (2%)
    dot_general x4, matrix products, atmos_core(): jnp.einsum('lm,vmxy->vlxy', levels, center, precision=lax.Precision.HIGHEST)  52.3 us
    ppermute x12, starting transfers between devices, padded_2(): lax.ppermute(lax.slice_in_dim(block, 0, width, axis=dim), axis, backward)  31.1 us
    ppermute x12, starting transfers between devices, padded_2(): lax.ppermute(lax.slice_in_dim(block, block.shape[dim] - width, None, axis...  24.4 us
    scatter x1, local copies, waits for them, and re-layouts, per_device(): outbox = jnp.zeros((devices * capacity, variables, 128), jnp.float32).at[...  24.1 us
    unnamed x24, local copies, waits for them, and re-layouts  14.3 us
    all_to_all x1, starting transfers between devices, per_device(): lax.all_to_all(outbox, ('grp', 'dom'), split_axis=0, concat_axis=0, tiled...  12.2 us
    ppermute x12, waiting for transfers between devices, padded_2(): lax.ppermute(lax.slice_in_dim(block, 0, width, axis=dim), axis, backward)  10.7 us
    dot_general x1, matrix products, per_device(): jnp.einsum('tfo,tao->tfa', flux_tiles, tile_weight, preferred_element_typ...  7.78 us
  transfers between devices with their start and end apart: 27, of which 5 were waited for; matrix products, arithmetic and copies ran while one was open for 44% of the time, Pallas kernels for 0%

commit v1 on v0

v1 whole, which is shorter than its diff:
```python
import functools

import jax
import jax.numpy as jnp
from jax import lax
from jax.experimental import pallas as pl
from jax.experimental.pallas import tpu as pltpu
from jax.sharding import PartitionSpec as P

STEPS = 4
MESH = pl.DeviceIdType.MESH
F32, BF16, I32 = jnp.float32, jnp.bfloat16, jnp.int32

diffuse = 0.2
vertical = 0.25
couple = 0.5


def split(x):
    hi = x.astype(BF16)
    return hi, (x - hi.astype(F32)).astype(BF16)


def dot(a, b):
    return jnp.dot(a, b, preferred_element_type=F32)


def exact_dot(a, b):
    return jnp.dot(a, b, preferred_element_type=F32, precision=lax.Precision.HIGHEST)


def level_terms(levels):
    lev = levels.shape[0]
    size = lev * 8
    spread = (
        lax.broadcasted_iota(I32, (size, lev), 0) // 8 == lax.broadcasted_iota(I32, (size, lev), 1)
    ).astype(F32)
    spread_t = (
        lax.broadcasted_iota(I32, (lev, size), 1) // 8 == lax.broadcasted_iota(I32, (lev, size), 0)
    ).astype(F32)
    wide = exact_dot(exact_dot(spread, vertical * levels), spread_t)
    same = lax.broadcasted_iota(I32, (size, size), 0) % 8 == lax.broadcasted_iota(I32, (size, size), 1) % 8
    k1 = jnp.where(same, wide, 0.0)
    k2 = exact_dot(k1, k1)
    k3 = exact_dot(k2, k1)
    k4 = exact_dot(k2, k2)
    hi, lo = split(jnp.concatenate([4.0 * k1, 6.0 * k2, 4.0 * k3, k4], axis=0))
    return jnp.concatenate([hi, hi, lo], axis=1)


def mix(lhs, cells):
    lev, _, n = cells.shape
    hi, lo = split(cells.reshape(lev * 8, n))
    out = dot(lhs, jnp.concatenate([hi, lo, hi], axis=0))
    return out.reshape(lhs.shape[0] // (lev * 8), lev, 8, n)


def pack_pairs(cells):
    n2, _, n = cells.shape
    pairs = cells.reshape(n2 // 2, 2, 8, n)
    a, b = pairs[:, 0], pairs[:, 1]
    upper = lax.broadcasted_iota(I32, a.shape, 1) < 4
    top = jnp.where(upper, a, pltpu.roll(b, 4, 1))
    bottom = jnp.where(upper, pltpu.roll(a, 4, 1), b)
    return top, bottom


def halo_pair(high, low):
    upper = lax.broadcasted_iota(I32, high.shape, 0) < 4
    first = jnp.where(upper, high, pltpu.roll(low, 4, 0))
    second = jnp.where(upper, pltpu.roll(high, 4, 0), low)
    return first, second


def spread_groups(rows):
    which = lax.broadcasted_iota(I32, rows.shape, 0) % 8
    return jnp.concatenate([jnp.where(which == t, rows, 0.0).astype(BF16) for t in range(8)], axis=1)


def body(
    grid_shape,
    w_hbm, atm_hbm, ocean_ref, alev_ref, olev_ref, owner_ref, block_ref, source_ref, count_ref,
    out_hbm, oout_ref,
    w, atm, res, halo_src, halo_dst, halo, terms,
    o_src, o_dst, os_src, os_dst, om_src, om_dst, oext, oterms, o_lhs, a_lhs,
    tiles_f, contrib, acc, acc_in, send2, inbox, flux_all, ret,
    w_sem, atm_sem, out_sem, h_send, h_recv, o_send, o_recv, p1_sem, p2_send, p2_recv, p3_send, p3_recv, p4_sem,
):
    n_grp, n_dom = grid_shape
    nv, lev, rows, cols = atm.shape
    tiles = w.shape[0]
    chunks = cols // 128
    half = n_dom // 2
    nc = n_grp * half
    obl = send2.shape[0] // nc
    orow = ocean_ref.shape[2]
    ocol = ocean_ref.shape[3]
    g, j = lax.axis_index("grp"), lax.axis_index("dom")
    me = g * n_dom + j
    core = lax.rem(j, 2)
    chip = g * half + j // 2
    total = n_grp * n_dom

    def flat(d):
        return (d // n_dom, lax.rem(d, n_dom))

    def peer(k):
        c = lax.rem(chip + k, nc)
        return c, (c // half, lax.rem(c, half) * 2 + core)

    right, left = flat(lax.rem(me + 1, total)), flat(lax.rem(me + total - 1, total))
    partner = (g, j + 1 - 2 * core)
    up, down = (g, lax.rem(j + n_dom - 1, n_dom)), (g, lax.rem(j + 1, n_dom))
    side, side_up, side_down = (1 - g, j), (1 - g, up[1]), (1 - g, down[1])

    parts = w_sem.shape[0]
    per = tiles // parts

    def w_copy(c):
        span = pl.ds(c * per, per)
        return pltpu.make_async_copy(w_hbm.at[span], w.at[span], w_sem.at[c])

    def atm_copy(v):
        return pltpu.make_async_copy(atm_hbm.at[v], atm.at[v], atm_sem.at[v])

    for v in range(nv):
        atm_copy(v).start()
    for c in range(parts):
        w_copy(c).start()

    barrier = pltpu.get_barrier_semaphore()
    for who in (right, left, up, down, side, side_up, side_down):
        pl.semaphore_signal(barrier, inc=1, device_id=who, device_id_type=MESH)

    def greet(k, carry):
        pl.semaphore_signal(barrier, inc=1, device_id=peer(k)[1], device_id_type=MESH)
        return carry

    lax.fori_loop(1, nc, greet, 0)

    ocean = ocean_ref[...].reshape(nv * lev, orow, ocol)
    otop, obottom = pack_pairs(ocean)
    pairs = nv * lev // 2
    o_src[0] = otop.reshape(pairs * 8, ocol).astype(BF16)
    o_src[1] = obottom.reshape(pairs * 8, ocol).astype(BF16)

    def edge(x):
        return jnp.where(g == 0, x[..., ocol - 128:], x[..., :128])

    os_src[0] = edge(otop).reshape(pairs * 8, 128).astype(BF16)
    os_src[1] = edge(obottom).reshape(pairs * 8, 128).astype(BF16)
    om_src[...] = edge(ocean).reshape(nv * lev * 8, 128).astype(BF16)

    pl.semaphore_wait(barrier, 7 + nc - 1)

    def remote(src, dst, ssem, rsem, who):
        return pltpu.make_async_remote_copy(
            src_ref=src, dst_ref=dst, send_sem=ssem, recv_sem=rsem, device_id=who, device_id_type=MESH
        )

    o_copies = [
        remote(o_src.at[0], o_dst.at[0], o_send.at[0], o_recv.at[0], up),
        remote(o_src.at[1], o_dst.at[1], o_send.at[1], o_recv.at[1], down),
        remote(os_src.at[0], os_dst.at[0], o_send.at[2], o_recv.at[2], side_up),
        remote(os_src.at[1], os_dst.at[1], o_send.at[3], o_recv.at[3], side_down),
        remote(om_src, om_dst, o_send.at[4], o_recv.at[4], side),
    ]
    for copy in o_copies:
        copy.start()

    for v in range(nv):
        atm_copy(v).wait()
    h_copies = [
        remote(halo_src.at[0], halo_dst.at[0], h_send.at[0], h_recv.at[0], left),
        remote(halo_src.at[1], halo_dst.at[1], h_send.at[1], h_recv.at[1], right),
    ]

    def pack_halo(i, carry):
        v, pair = i // (lev // 4), lax.rem(i, lev // 4) * 4
        top, _ = pack_pairs(atm[v, pl.ds(pair, 4), 0:8, :])
        _, bottom = pack_pairs(atm[v, pl.ds(pair, 4), rows - 8:rows, :])
        span = pl.ds(pl.multiple_of(i * 16, 16), 16)
        halo_src[0, span, :] = top.reshape(16, cols).astype(BF16)
        halo_src[1, span, :] = bottom.reshape(16, cols).astype(BF16)
        return carry

    lax.fori_loop(0, nv * lev // 4, pack_halo, 0)
    for copy in h_copies:
        copy.start()

    nch = ocol // 128
    live = lax.broadcasted_iota(I32, (1, tiles), 1) < count_ref[0]
    owner, block, source = owner_ref[...], block_ref[...], source_ref[...]
    dest = (owner & 1) * (nc * obl) + (owner >> 1) * obl
    dest = dest + (block & (nch - 1)) * orow + (block >> (nch.bit_length() - 1))
    dest = jnp.where(live, dest, -1)
    place = (source & (chunks - 1)) * rows + (source >> (chunks.bit_length() - 1))
    place = jnp.where(live, place, -1)
    eye = lax.broadcasted_iota(I32, (tiles, tiles), 0) == lax.broadcasted_iota(I32, (tiles, tiles), 1)

    def column(x):
        return jnp.sum(jnp.where(eye, x.astype(F32), 0.0), axis=1, keepdims=True).astype(I32)

    dest_col, place_col = column(dest), column(place)
    nblk = chunks * rows
    pick = (lax.broadcasted_iota(I32, (tiles, nblk), 1) == place_col).astype(F32).astype(BF16)

    def as_blocks(v):
        field = atm[v, 0]
        return jnp.concatenate([field[:, c * 128:(c + 1) * 128] for c in range(chunks)], axis=0)

    surface = jnp.concatenate([as_blocks(v) for v in range(nv)], axis=1).astype(BF16)

    def tile_rows(values):
        values = values.reshape(tiles // 8, 8, nv * 128)
        tiles_f[...] = jnp.concatenate([values[:, :, v * 128:(v + 1) * 128] for v in range(nv)], axis=1)

    tile_rows(dot(pick, surface))
    pairs16 = tiles // 16

    def keep(i, out):
        for h in range(2):
            part = out[h * 16:(h + 1) * 16, h * 128:(h + 1) * 128]
            span = pl.ds(pl.multiple_of(i * 16 + h * 8, 8), 8)
            contrib[span, 0:128] = part[0:8]
            contrib[span, 128:256] = part[8:16]

    def forward(c, carry):
        w_copy(c).wait()
        for s in range(per // 16):
            i = c * (per // 16) + s
            lhs = jnp.concatenate([spread_groups(tiles_f[2 * i]), spread_groups(tiles_f[2 * i + 1])], axis=0)
            both = w[pl.ds(i * 16, 16)].reshape(2, 1024, 128)
            keep(i, dot(lhs, jnp.concatenate([both[0], both[1]], axis=1)))
        return carry

    lax.fori_loop(0, parts, forward, 0)

    chi, clo = split(contrib[...])
    span = nc * obl
    for h in range(2):
        hot = (lax.broadcasted_iota(I32, (span, tiles), 0) + h * span == dest).astype(F32).astype(BF16)
        acc[h] = dot(hot, chi) + dot(hot, clo)
    p1 = remote(acc.at[1 - core], acc_in, p1_sem.at[0], p1_sem.at[1], partner)
    p1.start()
    o_lhs[...] = level_terms(olev_ref[...])
    p1.wait_recv()
    own = acc[core] + acc_in[...]
    send2[...] = own.astype(BF16)

    def slot(ref, c):
        return ref.at[pl.ds(pl.multiple_of(c * obl, obl), obl)]

    def p2(k):
        c, who = peer(k)
        return remote(slot(send2, c), slot(inbox, chip), p2_send.at[c], p2_recv.at[chip], who)

    def p2_in(k):
        c, who = peer(k)
        return remote(slot(send2, c), slot(inbox, c), p2_send.at[c], p2_recv.at[c], who)

    def loop(f):
        def step(k, carry):
            f(k)
            return carry

        lax.fori_loop(1, nc, step, 0)

    loop(lambda k: p2(k).start())
    a_lhs[...] = level_terms(alev_ref[...])

    width = 512

    def atm_terms(v, t, rows_of, lhs):
        kinds = lhs.shape[0] // (lev * 8)

        def one(c, carry):
            at = pl.ds(pl.multiple_of(c * width, width), width)
            terms[0:kinds, :, t * 8:(t + 1) * 8, at] = mix(lhs, rows_of(at))
            return carry

        lax.fori_loop(0, cols // width, one, 0)

    for t in range(rows // 8):
        atm_terms(0, t, lambda at: atm[0, :, t * 8:(t + 1) * 8, at], a_lhs[...])

    mine = pl.ds(pl.multiple_of(chip * obl, obl), obl)
    loop(lambda k: p2_in(k).wait_recv())
    inbox[mine, :] = send2[mine, :]
    received = jnp.sum(inbox[...].astype(F32).reshape(nc, obl, nv * 128), axis=0)
    osurf = [
        jnp.concatenate([ocean_ref[v, 0, :, c * 128:(c + 1) * 128] for c in range(nch)], axis=0) for v in range(nv)
    ]
    flux = received - jnp.concatenate(osurf, axis=1)
    flux_all[core, mine, :] = flux.astype(BF16)

    def p3(k):
        c, who = peer(k)
        return remote(slot(flux_all.at[core], chip), slot(flux_all.at[core], chip), p3_send.at[c], p3_recv.at[chip], who)

    def p3_in(k):
        c, who = peer(k)
        return remote(slot(flux_all.at[core], c), slot(flux_all.at[core], c), p3_send.at[c], p3_recv.at[c], who)

    loop(lambda k: p3(k).start())

    for copy in o_copies:
        copy.wait_recv()
    for v in range(nv):
        m = nv * lev // 2 // nv
        top = jnp.concatenate([o_dst[0], os_dst[0]], axis=1).astype(F32).reshape(pairs, 8, ocol + 128)
        bottom = jnp.concatenate([o_dst[1], os_dst[1]], axis=1).astype(F32).reshape(pairs, 8, ocol + 128)
        beside = om_dst[...].astype(F32).reshape(nv, lev, 8, 128)
        oext[:, 0:8, 0:ocol] = ocean_ref[v]
        oext[:, 0:8, ocol:] = beside[v]
        for q in range(m):
            first, second = halo_pair(top[v * m + q], bottom[v * m + q])
            oext[2 * q, 8:16, :] = first
            oext[2 * q + 1, 8:16, :] = second
        for t in range(2):
            oterms[:, :, t * 8:(t + 1) * 8, :] = mix(o_lhs[...], oext[:, t * 8:(t + 1) * 8, :])
        shape = (16, ocol + 128)
        r_at, c_at = lax.broadcasted_iota(I32, shape, 0), lax.broadcasted_iota(I32, shape, 1)
        no_up = (r_at == 0) & (j == 0)
        no_down = (r_at == 7) & (j == n_dom - 1)
        no_left = (c_at == 0) & (g == 0)
        no_right = (c_at == ocol - 1) & (g == n_grp - 1)

        def ocean_level(l, carry):
            r = oext[l]
            for k in range(STEPS):
                total4 = jnp.where(no_up, 0.0, pltpu.roll(r, 1, 0)) + jnp.where(no_down, 0.0, pltpu.roll(r, 15, 0))
                total4 = total4 + jnp.where(no_left, 0.0, pltpu.roll(r, 1, 1))
                total4 = total4 + jnp.where(no_right, 0.0, pltpu.roll(r, ocol + 127, 1))
                r = diffuse * (r + total4) + oterms[k, l]
            oout_ref[v, l] = r[0:8, 0:ocol]
            return carry

        lax.fori_loop(0, lev, ocean_level, 0)
        field = jnp.concatenate([flux[c * 8:(c + 1) * 8, v * 128:(v + 1) * 128] for c in range(nch)], axis=1)
        oout_ref[v, 0] = oout_ref[v, 0] + couple * field

    loop(lambda k: p3_in(k).wait_recv())
    p4 = remote(flux_all.at[core], flux_all.at[core], p4_sem.at[0], p4_sem.at[1], partner)
    p4_in = remote(flux_all.at[1 - core], flux_all.at[1 - core], p4_sem.at[0], p4_sem.at[1], partner)
    p4.start()

    for copy in h_copies:
        copy.wait_recv()
    zeros = jnp.zeros((rows + 8, 128), F32)

    def out_copy(v):
        return pltpu.make_async_copy(res.at[v], out_hbm.at[v], out_sem.at[v])

    for v in range(nv):
        def unpack(i, carry):
            at = pl.ds(pl.multiple_of((v * lev // 4 + i) * 16, 16), 16)
            high, low = halo_dst[0, at, :].astype(F32), halo_dst[1, at, :].astype(F32)
            for q in range(2):
                first, second = halo_pair(high[q * 8:(q + 1) * 8], low[q * 8:(q + 1) * 8])
                halo[4 * i + 2 * q] = first
                halo[4 * i + 2 * q + 1] = second
            return carry

        lax.fori_loop(0, lev // 4, unpack, 0)
        if v > 0:
            for t in range(rows // 8):
                atm_terms(v, t, lambda at: atm[v, :, t * 8:(t + 1) * 8, at], a_lhs[...])
        atm_terms(v, rows // 8, lambda at: halo[:, :, at], a_lhs[0:3 * lev * 8, :])

        def atm_level(l, carry):
            r = jnp.concatenate([atm[v, l], halo[l]], axis=0)
            for k in range(STEPS):
                padded = jnp.concatenate([r, zeros], axis=1)
                along_y = pltpu.roll(padded, 1, 1)[:, :cols] + pltpu.roll(padded, cols + 127, 1)[:, :cols]
                along_x = pltpu.roll(r, 1, 0) + pltpu.roll(r, rows + 7, 0)
                r = r + along_x + along_y
                if k < STEPS - 1:
                    r = diffuse * r + terms[k, l]
                else:
                    r = diffuse * r[0:rows] + terms[k, l, 0:rows, :]
            res[v, l] = r
            return carry

        lax.fori_loop(0, lev, atm_level, 0)

    p4_in.wait_recv()
    hot = (lax.broadcasted_iota(I32, (tiles, 2 * span), 1) == dest_col).astype(F32).astype(BF16)
    tile_rows(dot(hot, flux_all[...].reshape(2 * span, nv * 128)))

    def backward(i, carry):
        lhs = jnp.concatenate([spread_groups(tiles_f[2 * i]), spread_groups(tiles_f[2 * i + 1])], axis=0)
        both = w[pl.ds(i * 16, 16)]
        rhs = jnp.concatenate(
            [jnp.concatenate([both[h * 8 + t] for t in range(8)], axis=1) for h in range(2)], axis=0
        )
        keep(i, lax.dot_general(lhs, rhs, (((1,), (1,)), ((), ())), preferred_element_type=F32))
        return carry

    lax.fori_loop(0, pairs16, backward, 0)
    bhi, blo = split(contrib[...])
    to_block = (lax.broadcasted_iota(I32, (nblk, tiles), 0) == place).astype(F32).astype(BF16)
    ret[...] = dot(to_block, bhi) + dot(to_block, blo)
    for v in range(nv):
        field = jnp.concatenate(
            [ret[c * rows:(c + 1) * rows, v * 128:(v + 1) * 128] for c in range(chunks)], axis=1
        )
        res[v, 0] = res[v, 0] - couple * field
        out_copy(v).start()

    for copy in o_copies + h_copies + [p1, p4]:
        copy.wait_send()
    loop(lambda k: p2(k).wait_send())
    loop(lambda k: p3(k).wait_send())
    for v in range(nv):
        out_copy(v).wait()


def solution(mesh):
    n_grp, n_dom = mesh.shape["grp"], mesh.shape["dom"]
    nc = n_grp * n_dom // 2

    def per_device(
        atm_state, ocean_state, atm_levels, ocean_levels, tile_weight, tile_owner, tile_block, tile_source, tile_count
    ):
        nv, lev, rows, cols = atm_state.shape
        tiles = tile_weight.shape[0]
        orow, ocol = ocean_state.shape[2:]
        obl = orow * ocol // 128
        pairs = nv * lev // 2
        lanes = nv * 128
        dma = pltpu.SemaphoreType.DMA
        vmem = pl.BlockSpec(memory_space=pltpu.VMEM)
        hbm = pl.BlockSpec(memory_space=pl.ANY)
        return pl.pallas_call(
            functools.partial(body, (n_grp, n_dom)),
            out_shape=(
                jax.ShapeDtypeStruct(atm_state.shape, F32),
                jax.ShapeDtypeStruct(ocean_state.shape, F32),
            ),
            in_specs=[hbm, hbm, vmem, vmem, vmem, vmem, vmem, vmem, pl.BlockSpec(memory_space=pltpu.SMEM)],
            out_specs=(hbm, vmem),
            scratch_shapes=[
                pltpu.VMEM(tile_weight.shape, BF16),
                pltpu.VMEM(atm_state.shape, F32),
                pltpu.VMEM(atm_state.shape, F32),
                pltpu.VMEM((2, pairs * 8, cols), BF16),
                pltpu.VMEM((2, pairs * 8, cols), BF16),
                pltpu.VMEM((lev, 8, cols), F32),
                pltpu.VMEM((STEPS, lev, rows + 8, cols), F32),
                pltpu.VMEM((2, pairs * 8, ocol), BF16),
                pltpu.VMEM((2, pairs * 8, ocol), BF16),
                pltpu.VMEM((2, pairs * 8, 128), BF16),
                pltpu.VMEM((2, pairs * 8, 128), BF16),
                pltpu.VMEM((nv * lev * 8, 128), BF16),
                pltpu.VMEM((nv * lev * 8, 128), BF16),
                pltpu.VMEM((lev, 16, ocol + 128), F32),
                pltpu.VMEM((STEPS, lev, 16, ocol + 128), F32),
                pltpu.VMEM((STEPS * lev * 8, 3 * lev * 8), BF16),
                pltpu.VMEM((STEPS * lev * 8, 3 * lev * 8), BF16),
                pltpu.VMEM((tiles // 8, 8 * nv, 128), F32),
                pltpu.VMEM((tiles, lanes), F32),
                pltpu.VMEM((2, nc * obl, lanes), F32),
                pltpu.VMEM((nc * obl, lanes), F32),
                pltpu.VMEM((nc * obl, lanes), BF16),
                pltpu.VMEM((nc * obl, lanes), BF16),
                pltpu.VMEM((2, nc * obl, lanes), BF16),
                pltpu.VMEM((rows * cols // 128, lanes), F32),
                dma((8,)), dma((nv,)), dma((nv,)),
                dma((2,)), dma((2,)), dma((5,)), dma((5,)),
                dma((2,)), dma((nc,)), dma((nc,)), dma((nc,)), dma((nc,)), dma((2,)),
            ],
            compiler_params=pltpu.CompilerParams(
                collective_id=0, has_side_effects=True, vmem_limit_bytes=60 * 1024 * 1024
            ),
            cost_estimate=pl.CostEstimate(flops=8_000_000_000, bytes_accessed=17_000_000, transcendentals=0),
        )(
            tile_weight, atm_state, ocean_state, atm_levels, ocean_levels,
            tile_owner.reshape(1, tiles), tile_block.reshape(1, tiles), tile_source.reshape(1, tiles), tile_count,
        )

    in_specs = (
        P(None, None, ("grp", "dom"), None),
        P(None, None, "dom", "grp"),
        P(),
        P(),
        P(("grp", "dom"), None, None),
        P(("grp", "dom"), None),
        P(("grp", "dom")),
        P(("grp", "dom")),
        P(("grp", "dom")),
    )
    out_specs = (P(None, None, ("grp", "dom"), None), P(None, None, "dom", "grp"))
    return jax.shard_map(per_device, mesh=mesh, in_specs=in_specs, out_specs=out_specs, check_vma=False)
```

time: 221 us -> 76.4 us (0.35)
  starting transfers between devices: 73.9 us -> 0 us
  Pallas kernels: 0 us -> 69.5 us
  matrix products: 68 us -> 0 us
  local copies, waits for them, and re-layouts: 57.2 us -> 5.45 us
  waiting for transfers between devices: 15 us -> 0 us
  other arithmetic: 3.81 us -> 0 us
    pallas_call x0 -> x1, Pallas kernels: none -> 69.5 us  [per_device(): pl.pallas_call(functools.partial(body, (n_grp, n_dom)), out_shape=(jax.Sh...]
    dot_general x12 -> x0, matrix products: 68 us -> none  [the longest x4 52.3 us: atmos_core(): jnp.einsum('lm,vmxy->vlxy', levels, center, precision=lax.Precision.HIGHEST)]
    ppermute x24 -> x0, starting transfers between devices: 55.5 us -> none  [the longest x12 31.1 us: padded_2(): lax.ppermute(lax.slice_in_dim(block, 0, width, axis=dim), axis, backward)]
    scatter x2 -> x0, local copies, waits for them, and re-layouts: 25.7 us -> none  [the longest x1 24.1 us: per_device(): outbox = jnp.zeros((devices * capacity, variables, 128), jnp.float32).at[...]
    all_to_all x3 -> x0, starting transfers between devices: 18.4 us -> none  [the longest x1 12.2 us: per_device(): lax.all_to_all(outbox, ('grp', 'dom'), split_axis=0, concat_axis=0, tiled...]
    ppermute x24 -> x0, waiting for transfers between devices: 15 us -> none  [the longest x12 10.7 us: padded_2(): lax.ppermute(lax.slice_in_dim(block, 0, width, axis=dim), axis, backward)]
    unnamed x24 -> x4, local copies, waits for them, and re-layouts: 14.3 us -> 5.45 us
    gather x4 -> x0, local copies, waits for them, and re-layouts: 6.57 us -> none  [the longest x1 2.37 us: per_device(): tile_rank = jnp.take_along_axis(order_rank, target[:, None], axis=1)[:, 0]]
  transfers between devices with their start and end apart: 27 -> 0, of which waited for: 5 -> 0; matrix products, arithmetic and copies ran while one was open for 44% -> 0% of each run, Pallas kernels for 0% -> 0%
where the time goes in v1:
time: 76.4 us; the launch traced here: 76.3 us
  Pallas kernels  69.5 us (91%)
  local copies, waits for them, and re-layouts  5.45 us (7%)
  between operations  1.3 us (2%)
    pallas_call x1, Pallas kernels, per_device(): pl.pallas_call(functools.partial(body, (n_grp, n_dom)), out_shape=(jax.Sh...  69.5 us
    unnamed x4, local copies, waits for them, and re-layouts  5.45 us

profile of v1, /device:TPU:0, one launch (start us, length us, event | category | flops | bytes accessed | tf_op | source)
XLA Modules:
  0.0 76.3 jit_solution(7150644418351172105)
XLA Ops:
  1.3 69.5 %shard_map.104 = (f32[2,16,16,2048]{3,2,1,0:T(8,128)}, f32[2,16,8,256]{3,2,1,0:T(8,128)}) custom-call(bf16[256,128,128]{2,1,0:T(8,128)(2,1)} %w_hbm.1, f32[2,16,16,2048]{3,2,1,0:T(8,128)} %atm_hbm.1, f32[2,16,8,256]{3,2,1,0:T(8,128)} %ocean_ref.1, f32[16,16]{1,0:T(8,128)} %alev_ref.1, f32[16,16]{1,0:T(8,128)} %olev_ref.1, s32[1,256]{1,0:T(1,128)} %bitcast.3, ...), custom_call_target="tpu_custom_call" | custom-call | flops 8000000000 | bytes 17000000 | tf_op jit(solution)/shard_map/pallas_call | solution.py:435
  70.8 0.0 copy-start
  70.8 4.7 %copy.14 = f32[2,16,16,2048]{3,2,1,0:T(8,128)} copy(f32[2,16,16,2048]{3,2,1,0:T(8,128)} %get-tuple-element.4) | data formatting | bytes 8388608
  75.6 0.0 copy-done
  75.6 0.7 copy.15
Async XLA Ops:
  70.8 4.8 %copy-start = (f32[2,16,8,256]{3,2,1,0:T(8,128)S(1)}, f32[2,16,8,256]{3,2,1,0:T(8,128)}, u32[]{:S(2)}) copy-start(f32[2,16,8,256]{3,2,1,0:T(8,128)} %get-tuple-element.5) | copy-start | bytes 786436

commit v2 on v1

--- a/solution.py
+++ b/solution.py
@@ -55,6 +55,66 @@
     return out.reshape(lhs.shape[0] // (lev * 8), lev, 8, n)
 
 
+BANDS = ((1,), (1, 1), (3, 2, 1), (7, 6, 3, 1), (19, 16, 10, 4, 1))
+CHOOSE = ((1,), (1, 1), (1, 2, 1), (1, 3, 3, 1), (1, 4, 6, 4, 1))
+
+
+def strip_operator(out_ref, levels, rows):
+    lev = levels.shape[0]
+    ext = rows + 8
+    size = lev * rows
+    power = [None, vertical * levels]
+    for n in range(2, STEPS + 1):
+        power.append(exact_dot(power[n - 1], power[1]))
+    spread = (
+        lax.broadcasted_iota(I32, (size, lev), 0) // rows == lax.broadcasted_iota(I32, (size, lev), 1)
+    ).astype(F32)
+    tall = [None] + [exact_dot(spread, p) for p in power[1:]]
+    base = 0
+    for per, first, times in ((rows, 0, 2), (8, rows, 1)):
+        n_col = lev * per
+        spread_c = (
+            lax.broadcasted_iota(I32, (lev, n_col), 1) // per == lax.broadcasted_iota(I32, (lev, n_col), 0)
+        ).astype(F32)
+        wide = [exact_dot(spread, spread_c)] + [exact_dot(p, spread_c) for p in tall[1:]]
+        x = lax.broadcasted_iota(I32, (size, n_col), 0) % rows
+        x_in = lax.broadcasted_iota(I32, (size, n_col), 1) % per + first
+        apart = jnp.abs(x_in - x)
+        apart = jnp.minimum(apart, ext - apart)
+        band = []
+        for m in range(STEPS + 1):
+            value = jnp.zeros((size, n_col), F32)
+            for d in range(m + 1):
+                value = jnp.where(apart == d, diffuse ** m * BANDS[m][d], value)
+            band.append(value)
+        for k in range(STEPS):
+            n = STEPS - k
+            value = jnp.zeros((size, n_col), F32)
+            for i in range(n + 1):
+                value = value + CHOOSE[n][i] * band[n - i] * wide[i]
+            hi, lo = split(CHOOSE[STEPS][k] * diffuse ** k * value)
+            at = pl.ds(k * size, size)
+            for copy in range(times):
+                out_ref[at, base + copy * n_col:base + (copy + 1) * n_col] = hi
+            out_ref[at, base + times * n_col:base + (times + 1) * n_col] = lo
+        base = base + (times + 1) * n_col
+
+
+def tile_map(tiles, count, owner, block, source, span, obl, orow, nch, rows, chunks):
+    live = lax.broadcasted_iota(I32, (1, tiles), 1) < count
+    dest = (owner & 1) * span + (owner >> 1) * obl
+    dest = dest + (block & (nch - 1)) * orow + (block >> (nch.bit_length() - 1))
+    dest = jnp.where(live, dest, -1)
+    place = (source & (chunks - 1)) * rows + (source >> (chunks.bit_length() - 1))
+    place = jnp.where(live, place, -1)
+    eye = lax.broadcasted_iota(I32, (tiles, tiles), 0) == lax.broadcasted_iota(I32, (tiles, tiles), 1)
+
+    def column(x):
+        return jnp.sum(jnp.where(eye, x.astype(F32), 0.0), axis=1, keepdims=True).astype(I32)
+
+    return dest, place, column(dest), column(place)
+
+
 def pack_pairs(cells):
     n2, _, n = cells.shape
     pairs = cells.reshape(n2 // 2, 2, 8, n)
@@ -80,10 +140,10 @@
 def body(
     grid_shape,
     w_hbm, atm_hbm, ocean_ref, alev_ref, olev_ref, owner_ref, block_ref, source_ref, count_ref,
-    out_hbm, oout_ref,
+    out_hbm, oout_ref, flux_ref,
     w, atm, res, halo_src, halo_dst, halo, terms,
     o_src, o_dst, os_src, os_dst, om_src, om_dst, oext, oterms, o_lhs, a_lhs,
-    tiles_f, contrib, acc, acc_in, send2, inbox, flux_all, ret,
+    tiles_f, contrib, acc, acc_in, send2, inbox, flux_all,
     w_sem, atm_sem, out_sem, h_send, h_recv, o_send, o_recv, p1_sem, p2_send, p2_recv, p3_send, p3_recv, p4_sem,
 ):
     n_grp, n_dom = grid_shape
@@ -189,19 +249,10 @@
         copy.start()
 
     nch = ocol // 128
-    live = lax.broadcasted_iota(I32, (1, tiles), 1) < count_ref[0]
-    owner, block, source = owner_ref[...], block_ref[...], source_ref[...]
-    dest = (owner & 1) * (nc * obl) + (owner >> 1) * obl
-    dest = dest + (block & (nch - 1)) * orow + (block >> (nch.bit_length() - 1))
-    dest = jnp.where(live, dest, -1)
-    place = (source & (chunks - 1)) * rows + (source >> (chunks.bit_length() - 1))
-    place = jnp.where(live, place, -1)
-    eye = lax.broadcasted_iota(I32, (tiles, tiles), 0) == lax.broadcasted_iota(I32, (tiles, tiles), 1)
-
-    def column(x):
-        return jnp.sum(jnp.where(eye, x.astype(F32), 0.0), axis=1, keepdims=True).astype(I32)
-
-    dest_col, place_col = column(dest), column(place)
+    span = nc * obl
+    dest, _, _, place_col = tile_map(
+        tiles, count_ref[0], owner_ref[...], block_ref[...], source_ref[...], span, obl, orow, nch, rows, chunks
+    )
     nblk = chunks * rows
     pick = (lax.broadcasted_iota(I32, (tiles, nblk), 1) == place_col).astype(F32).astype(BF16)
 
@@ -216,14 +267,13 @@
         tiles_f[...] = jnp.concatenate([values[:, :, v * 128:(v + 1) * 128] for v in range(nv)], axis=1)
 
     tile_rows(dot(pick, surface))
-    pairs16 = tiles // 16
 
     def keep(i, out):
         for h in range(2):
             part = out[h * 16:(h + 1) * 16, h * 128:(h + 1) * 128]
-            span = pl.ds(pl.multiple_of(i * 16 + h * 8, 8), 8)
-            contrib[span, 0:128] = part[0:8]
-            contrib[span, 128:256] = part[8:16]
+            at = pl.ds(pl.multiple_of(i * 16 + h * 8, 8), 8)
+            contrib[at, 0:128] = part[0:8]
+            contrib[at, 128:256] = part[8:16]
 
     def forward(c, carry):
         w_copy(c).wait()
@@ -237,13 +287,13 @@
     lax.fori_loop(0, parts, forward, 0)
 
     chi, clo = split(contrib[...])
-    span = nc * obl
     for h in range(2):
         hot = (lax.broadcasted_iota(I32, (span, tiles), 0) + h * span == dest).astype(F32).astype(BF16)
         acc[h] = dot(hot, chi) + dot(hot, clo)
     p1 = remote(acc.at[1 - core], acc_in, p1_sem.at[0], p1_sem.at[1], partner)
     p1.start()
     o_lhs[...] = level_terms(olev_ref[...])
+    strip_operator(a_lhs, alev_ref[...], rows)
     p1.wait_recv()
     own = acc[core] + acc_in[...]
     send2[...] = own.astype(BF16)
@@ -267,43 +317,6 @@
         lax.fori_loop(1, nc, step, 0)
 
     loop(lambda k: p2(k).start())
-    a_lhs[...] = level_terms(alev_ref[...])
-
-    width = 512
-
-    def atm_terms(v, t, rows_of, lhs):
-        kinds = lhs.shape[0] // (lev * 8)
-
-        def one(c, carry):
-            at = pl.ds(pl.multiple_of(c * width, width), width)
-            terms[0:kinds, :, t * 8:(t + 1) * 8, at] = mix(lhs, rows_of(at))
-            return carry
-
-        lax.fori_loop(0, cols // width, one, 0)
-
-    for t in range(rows // 8):
-        atm_terms(0, t, lambda at: atm[0, :, t * 8:(t + 1) * 8, at], a_lhs[...])
-
-    mine = pl.ds(pl.multiple_of(chip * obl, obl), obl)
-    loop(lambda k: p2_in(k).wait_recv())
-    inbox[mine, :] = send2[mine, :]
-    received = jnp.sum(inbox[...].astype(F32).reshape(nc, obl, nv * 128), axis=0)
-    osurf = [
-        jnp.concatenate([ocean_ref[v, 0, :, c * 128:(c + 1) * 128] for c in range(nch)], axis=0) for v in range(nv)
-    ]
-    flux = received - jnp.concatenate(osurf, axis=1)
-    flux_all[core, mine, :] = flux.astype(BF16)
-
-    def p3(k):
-        c, who = peer(k)
-        return remote(slot(flux_all.at[core], chip), slot(flux_all.at[core], chip), p3_send.at[c], p3_recv.at[chip], who)
-
-    def p3_in(k):
-        c, who = peer(k)
-        return remote(slot(flux_all.at[core], c), slot(flux_all.at[core], c), p3_send.at[c], p3_recv.at[c], who)
-
-    loop(lambda k: p3(k).start())
-
     for copy in o_copies:
         copy.wait_recv()
     for v in range(nv):
@@ -337,20 +350,44 @@
             return carry
 
         lax.fori_loop(0, lev, ocean_level, 0)
+    mine = pl.ds(pl.multiple_of(chip * obl, obl), obl)
+    loop(lambda k: p2_in(k).wait_recv())
+    inbox[mine, :] = send2[mine, :]
+    received = jnp.sum(inbox[...].astype(F32).reshape(nc, obl, nv * 128), axis=0)
+    osurf = [
+        jnp.concatenate([ocean_ref[v, 0, :, c * 128:(c + 1) * 128] for c in range(nch)], axis=0) for v in range(nv)
+    ]
+    flux = received - jnp.concatenate(osurf, axis=1)
+    flux_all[core, mine, :] = flux.astype(BF16)
+
+    def p3(k):
+        c, who = peer(k)
+        return remote(slot(flux_all.at[core], chip), slot(flux_all.at[core], chip), p3_send.at[c], p3_recv.at[chip], who)
+
+    def p3_in(k):
+        c, who = peer(k)
+        return remote(slot(flux_all.at[core], c), slot(flux_all.at[core], c), p3_send.at[c], p3_recv.at[c], who)
+
+    loop(lambda k: p3(k).start())
+
+    for v in range(nv):
         field = jnp.concatenate([flux[c * 8:(c + 1) * 8, v * 128:(v + 1) * 128] for c in range(nch)], axis=1)
         oout_ref[v, 0] = oout_ref[v, 0] + couple * field
 
-    loop(lambda k: p3_in(k).wait_recv())
+    for copy in h_copies:
+        copy.wait_recv()
+    zeros = jnp.zeros((rows, 128), F32)
+    width = 512
+
+    def out_copy(v):
+        return pltpu.make_async_copy(res.at[v], out_hbm.at[v], out_sem.at[v])
+
+    def along_y(r):
+        padded = jnp.concatenate([r, zeros], axis=1)
+        return pltpu.roll(padded, 1, 1)[:, :cols] + pltpu.roll(padded, cols + 127, 1)[:, :cols]
+
     p4 = remote(flux_all.at[core], flux_all.at[core], p4_sem.at[0], p4_sem.at[1], partner)
     p4_in = remote(flux_all.at[1 - core], flux_all.at[1 - core], p4_sem.at[0], p4_sem.at[1], partner)
-    p4.start()
-
-    for copy in h_copies:
-        copy.wait_recv()
-    zeros = jnp.zeros((rows + 8, 128), F32)
-
-    def out_copy(v):
-        return pltpu.make_async_copy(res.at[v], out_hbm.at[v], out_sem.at[v])
 
     for v in range(nv):
         def unpack(i, carry):
@@ -363,57 +400,143 @@
             return carry
 
         lax.fori_loop(0, lev // 4, unpack, 0)
-        if v > 0:
-            for t in range(rows // 8):
-                atm_terms(v, t, lambda at: atm[v, :, t * 8:(t + 1) * 8, at], a_lhs[...])
-        atm_terms(v, rows // 8, lambda at: halo[:, :, at], a_lhs[0:3 * lev * 8, :])
+
+        def along_levels(c, carry):
+            at = pl.ds(pl.multiple_of(c * width, width), width)
+            hi, lo = split(atm[v, :, :, at].reshape(lev * rows, width))
+            beyond = halo[:, :, at].reshape(lev * 8, width).astype(BF16)
+            out = dot(a_lhs[...], jnp.concatenate([hi, lo, hi, beyond, beyond], axis=0))
+            terms[:, :, :, at] = out.reshape(STEPS, lev, rows, width)
+            return carry
+
+        lax.fori_loop(0, cols // width, along_levels, 0)
 
         def atm_level(l, carry):
-            r = jnp.concatenate([atm[v, l], halo[l]], axis=0)
-            for k in range(STEPS):
-                padded = jnp.concatenate([r, zeros], axis=1)
-                along_y = pltpu.roll(padded, 1, 1)[:, :cols] + pltpu.roll(padded, cols + 127, 1)[:, :cols]
-                along_x = pltpu.roll(r, 1, 0) + pltpu.roll(r, rows + 7, 0)
-                r = r + along_x + along_y
-                if k < STEPS - 1:
-                    r = diffuse * r + terms[k, l]
-                else:
-                    r = diffuse * r[0:rows] + terms[k, l, 0:rows, :]
+            r = diffuse ** STEPS * atm[v, l]
+            for k in range(STEPS - 1, -1, -1):
+                r = terms[k, l] + along_y(r)
             res[v, l] = r
             return carry
 
         lax.fori_loop(0, lev, atm_level, 0)
+        out_copy(v).start()
+        if v == 0:
+            loop(lambda k: p3_in(k).wait_recv())
+            p4.start()
 
     p4_in.wait_recv()
-    hot = (lax.broadcasted_iota(I32, (tiles, 2 * span), 1) == dest_col).astype(F32).astype(BF16)
-    tile_rows(dot(hot, flux_all[...].reshape(2 * span, nv * 128)))
-
-    def backward(i, carry):
-        lhs = jnp.concatenate([spread_groups(tiles_f[2 * i]), spread_groups(tiles_f[2 * i + 1])], axis=0)
-        both = w[pl.ds(i * 16, 16)]
-        rhs = jnp.concatenate(
-            [jnp.concatenate([both[h * 8 + t] for t in range(8)], axis=1) for h in range(2)], axis=0
-        )
-        keep(i, lax.dot_general(lhs, rhs, (((1,), (1,)), ((), ())), preferred_element_type=F32))
-        return carry
-
-    lax.fori_loop(0, pairs16, backward, 0)
-    bhi, blo = split(contrib[...])
-    to_block = (lax.broadcasted_iota(I32, (nblk, tiles), 0) == place).astype(F32).astype(BF16)
-    ret[...] = dot(to_block, bhi) + dot(to_block, blo)
-    for v in range(nv):
-        field = jnp.concatenate(
-            [ret[c * rows:(c + 1) * rows, v * 128:(v + 1) * 128] for c in range(chunks)], axis=1
-        )
-        res[v, 0] = res[v, 0] - couple * field
-        out_copy(v).start()
-
+    flux_ref[...] = flux_all[...].reshape(2 * span, nv * 128)
     for copy in o_copies + h_copies + [p1, p4]:
         copy.wait_send()
     loop(lambda k: p2(k).wait_send())
     loop(lambda k: p3(k).wait_send())
     for v in range(nv):
         out_copy(v).wait()
+
+
+def back_body(
+    obl, orow, nch,
+    w_hbm, pre_hbm, opre_hbm, flux_ref, owner_ref, block_ref, source_ref, count_ref,
+    out_hbm, oout_hbm,
+    w, pre, opre, acc, contrib, ret,
+    w_sem, in_sem, out_sem, o_sem,
+):
+    nv, lev, rows, cols = pre.shape
+    tiles = w.shape[0]
+    chunks = cols // 128
+    span = flux_ref.shape[0] // 2
+    half = w_sem.shape[0]
+    per = tiles // half
+
+    def w_copy(c):
+        at = pl.ds(c * per, per)
+        return pltpu.make_async_copy(w_hbm.at[at], w.at[at], w_sem.at[c])
+
+    def first_in(v):
+        return pltpu.make_async_copy(pre_hbm.at[v, 0], pre.at[v, 0], in_sem.at[v, 0])
+
+    def rest_in(v):
+        at = pl.ds(1, lev - 1)
+        return pltpu.make_async_copy(pre_hbm.at[v, at], pre.at[v, at], in_sem.at[v, 1])
+
+    def first_out(v):
+        return pltpu.make_async_copy(pre.at[v, 0], out_hbm.at[v, 0], out_sem.at[v, 0])
+
+    def rest_out(v):
+        at = pl.ds(1, lev - 1)
+        return pltpu.make_async_copy(pre.at[v, at], out_hbm.at[v, at], out_sem.at[v, 1])
+
+    o_in = pltpu.make_async_copy(opre_hbm, opre, o_sem.at[0])
+    o_out = pltpu.make_async_copy(opre, oout_hbm, o_sem.at[1])
+    for c in range(half):
+        w_copy(c).start()
+    o_in.start()
+    for v in range(nv):
+        rest_in(v).start()
+        first_in(v).start()
+
+    _, place, dest_col, _ = tile_map(
+        tiles, count_ref[0], owner_ref[...], block_ref[...], source_ref[...], span, obl, orow, nch, rows, chunks
+    )
+    hot = (lax.broadcasted_iota(I32, (tiles, 2 * span), 1) == dest_col).astype(F32).astype(BF16)
+    values = dot(hot, flux_ref[...])
+    column = lax.broadcasted_iota(I32, (128, 256), 1) % 64
+    step = 4
+    blank = jnp.zeros((128, 128), BF16)
+    for q in range(tiles // 128):
+        groups = []
+        for h in range(2):
+            at = q * 128 + h * 64
+            both = jnp.concatenate([values[at:at + 64, v * 128:(v + 1) * 128] for v in range(nv)], axis=0)
+            groups.append(both.T.astype(BF16))
+        rhs = jnp.concatenate(
+            [
+                jnp.concatenate([groups[0], blank], axis=1),
+                jnp.concatenate([blank, groups[1]], axis=1),
+            ],
+            axis=0,
+        )
+        for c in range(q * half * 128 // tiles, (q + 1) * half * 128 // tiles):
+            w_copy(c).wait()
+        acc[...] = jnp.zeros((128, 256), F32)
+
+        def some(i, carry):
+            first = w[pl.ds(q * 128 + i * step, step)].reshape(step * 128, 128)
+            second = w[pl.ds(q * 128 + 64 + i * step, step)].reshape(step * 128, 128)
+            out = dot(jnp.concatenate([first, second], axis=1), rhs)
+            total = acc[...]
+            for t in range(step):
+                total = jnp.where(column == i * step + t, out[t * 128:(t + 1) * 128], total)
+            acc[...] = total
+            return carry
+
+        lax.fori_loop(0, 64 // step, some, 0)
+        turned = acc[...].T
+        for h in range(2):
+            for v in range(nv):
+                at = h * 128 + v * 64
+                contrib[q * 128 + h * 64:q * 128 + (h + 1) * 64, v * 128:(v + 1) * 128] = turned[at:at + 64]
+        if q == 0:
+            o_in.wait()
+            o_out.start()
+            for v in range(nv):
+                rest_in(v).wait()
+                rest_out(v).start()
+
+    bhi, blo = split(contrib[...])
+    to_block = (lax.broadcasted_iota(I32, (chunks * rows, tiles), 0) == place).astype(F32).astype(BF16)
+    ret[...] = dot(to_block, bhi) + dot(to_block, blo)
+    for v in range(nv):
+        first_in(v).wait()
+        field = jnp.concatenate(
+            [ret[c * rows:(c + 1) * rows, v * 128:(v + 1) * 128] for c in range(chunks)], axis=1
+        )
+        pre[v, 0] = pre[v, 0] - couple * field
+        first_out(v).start()
+    o_out.wait()
+    for v in range(nv):
+        rest_out(v).wait()
+        first_out(v).wait()
 
 
 def solution(mesh):
@@ -432,14 +555,20 @@
         dma = pltpu.SemaphoreType.DMA
         vmem = pl.BlockSpec(memory_space=pltpu.VMEM)
         hbm = pl.BlockSpec(memory_space=pl.ANY)
-        return pl.pallas_call(
+        tile_args = (
+            tile_owner.reshape(1, tiles), tile_block.reshape(1, tiles), tile_source.reshape(1, tiles), tile_count
+        )
+        smem = pl.BlockSpec(memory_space=pltpu.SMEM)
+        span = nc * obl
+        atm_pre, ocean_pre, flux = pl.pallas_call(
             functools.partial(body, (n_grp, n_dom)),
             out_shape=(
                 jax.ShapeDtypeStruct(atm_state.shape, F32),
                 jax.ShapeDtypeStruct(ocean_state.shape, F32),
+                jax.ShapeDtypeStruct((2 * span, lanes), BF16),
             ),
-            in_specs=[hbm, hbm, vmem, vmem, vmem, vmem, vmem, vmem, pl.BlockSpec(memory_space=pltpu.SMEM)],
-            out_specs=(hbm, vmem),
+            in_specs=[hbm, hbm, vmem, vmem, vmem, vmem, vmem, vmem, smem],
+            out_specs=(hbm, vmem, vmem),
             scratch_shapes=[
                 pltpu.VMEM(tile_weight.shape, BF16),
                 pltpu.VMEM(atm_state.shape, F32),
@@ -447,7 +576,7 @@
                 pltpu.VMEM((2, pairs * 8, cols), BF16),
                 pltpu.VMEM((2, pairs * 8, cols), BF16),
                 pltpu.VMEM((lev, 8, cols), F32),
-                pltpu.VMEM((STEPS, lev, rows + 8, cols), F32),
+                pltpu.VMEM((STEPS, lev, rows, cols), F32),
                 pltpu.VMEM((2, pairs * 8, ocol), BF16),
                 pltpu.VMEM((2, pairs * 8, ocol), BF16),
                 pltpu.VMEM((2, pairs * 8, 128), BF16),
@@ -457,7 +586,7 @@
                 pltpu.VMEM((lev, 16, ocol + 128), F32),
                 pltpu.VMEM((STEPS, lev, 16, ocol + 128), F32),
                 pltpu.VMEM((STEPS * lev * 8, 3 * lev * 8), BF16),
-                pltpu.VMEM((STEPS * lev * 8, 3 * lev * 8), BF16),
+                pltpu.VMEM((STEPS * lev * rows, 3 * lev * rows + 2 * lev * 8), BF16),
                 pltpu.VMEM((tiles // 8, 8 * nv, 128), F32),
                 pltpu.VMEM((tiles, lanes), F32),
                 pltpu.VMEM((2, nc * obl, lanes), F32),
@@ -465,7 +594,6 @@
                 pltpu.VMEM((nc * obl, lanes), BF16),
                 pltpu.VMEM((nc * obl, lanes), BF16),
                 pltpu.VMEM((2, nc * obl, lanes), BF16),
-                pltpu.VMEM((rows * cols // 128, lanes), F32),
                 dma((8,)), dma((nv,)), dma((nv,)),
                 dma((2,)), dma((2,)), dma((5,)), dma((5,)),
                 dma((2,)), dma((nc,)), dma((nc,)), dma((nc,)), dma((nc,)), dma((2,)),
@@ -475,9 +603,28 @@
             ),
             cost_estimate=pl.CostEstimate(flops=8_000_000_000, bytes_accessed=17_000_000, transcendentals=0),
         )(
-            tile_weight, atm_state, ocean_state, atm_levels, ocean_levels,
-            tile_owner.reshape(1, tiles), tile_block.reshape(1, tiles), tile_source.reshape(1, tiles), tile_count,
+            tile_weight, atm_state, ocean_state, atm_levels, ocean_levels, *tile_args
         )
+        return pl.pallas_call(
+            functools.partial(back_body, obl, orow, ocol // 128),
+            out_shape=(
+                jax.ShapeDtypeStruct(atm_state.shape, F32),
+                jax.ShapeDtypeStruct(ocean_state.shape, F32),
+            ),
+            in_specs=[hbm, hbm, hbm, vmem, vmem, vmem, vmem, smem],
+            out_specs=(hbm, hbm),
+            scratch_shapes=[
+                pltpu.VMEM(tile_weight.shape, BF16),
+                pltpu.VMEM(atm_state.shape, F32),
+                pltpu.VMEM(ocean_state.shape, F32),
+                pltpu.VMEM((128, 256), F32),
+                pltpu.VMEM((tiles, lanes), F32),
+                pltpu.VMEM((rows * cols // 128, lanes), F32),
+                dma((4,)), dma((nv, 2)), dma((nv, 2)), dma((2,)),
+            ],
+            compiler_params=pltpu.CompilerParams(vmem_limit_bytes=40 * 1024 * 1024),
+            cost_estimate=pl.CostEstimate(flops=2_000_000_000, bytes_accessed=17_000_000, transcendentals=0),
+        )(tile_weight, atm_pre, ocean_pre, flux, *tile_args)
 
     in_specs = (
         P(None, None, ("grp", "dom"), None),

time: 76.4 us -> 75.2 us (0.984); the launches traced: 76.3 us -> 73.9 us
  Pallas kernels: 69.5 us -> 65.1 us
  local copies, waits for them, and re-layouts: 5.45 us -> 7.48 us
    pallas_call x1, Pallas kernels: 69.5 us -> 54.5 us  [per_device(): pl.pallas_call(functools.partial(body, (n_grp, n_dom)), out_shape=(jax.Sh...]
    pallas_call x0 -> x1, Pallas kernels: none -> 10.6 us  [per_device(): pl.pallas_call(functools.partial(back_body, obl, orow, ocol // 128), out_...]
    unnamed x4 -> x14, local copies, waits for them, and re-layouts: 5.45 us -> 7.48 us
where the time goes in v2:
time: 75.2 us; the launch traced here: 73.9 us
  Pallas kernels  65.1 us (87%)
  local copies, waits for them, and re-layouts  7.48 us (10%)
  between operations  1.35 us (2%)
    pallas_call x1, Pallas kernels, per_device(): pl.pallas_call(functools.partial(body, (n_grp, n_dom)), out_shape=(jax.Sh...  54.5 us
    pallas_call x1, Pallas kernels, per_device(): pl.pallas_call(functools.partial(back_body, obl, orow, ocol // 128), out_...  10.6 us
    unnamed x14, local copies, waits for them, and re-layouts  7.48 us

profile of v2, /device:TPU:0, one launch (start us, length us, event | category | flops | bytes accessed | tf_op | source)
XLA Modules:
  0.0 73.9 jit_solution(15752035445418056650)
XLA Ops:
  1.3 0.0 copy-start.4
  1.3 0.0 copy-start.5
  1.3 0.0 copy-start.6
  1.3 54.5 %shard_map.104 = (f32[2,16,16,2048]{3,2,1,0:T(8,128)}, f32[2,16,8,256]{3,2,1,0:T(8,128)}, bf16[512,256]{1,0:T(8,128)(2,1)}) custom-call(bf16[256,128,128]{2,1,0:T(8,128)(2,1)} %w_hbm.3, f32[2,16,16,2048]{3,2,1,0:T(8,128)} %atm_hbm.1, f32[2,16,8,256]{3,2,1,0:T(8,128)} %ocean_ref.1, f32[16,16]{1,0:T(8,128)} %alev_ref.1, f32[16,16]{1,0:T(8,128)} %olev_ref.1, ...), custom_call_target="tpu_custom_call" | custom-call | flops 8000000000 | bytes 17000000 | tf_op jit(solution)/shard_map/pallas_call | solution.py:563
  55.9 0.0 copy-done.4
  55.9 0.0 copy-done.5
  55.9 0.0 copy-done.6
  55.9 0.0 copy-start
  55.9 3.4 %copy-done = bf16[256,128,128]{2,1,0:T(8,128)(2,1)S(1)} copy-done((bf16[256,128,128]{2,1,0:T(8,128)(2,1)S(1)}, bf16[256,128,128]{2,1,0:T(8,128)(2,1)}, u32[]{:S(2)}) %copy-start) | copy-done | bytes 8388632
  59.3 0.0 copy-start.1
  59.3 2.2 %copy-done.1 = f32[2,16,16,2048]{3,2,1,0:T(8,128)S(1)} copy-done((f32[2,16,16,2048]{3,2,1,0:T(8,128)S(1)}, f32[2,16,16,2048]{3,2,1,0:T(8,128)}, u32[]{:S(2)}) %copy-start.1) | copy-done | bytes 4194328
  61.5 0.0 copy-start.2
  61.5 0.9 %copy-done.2 = f32[2,16,8,256]{3,2,1,0:T(8,128)S(1)} copy-done((f32[2,16,8,256]{3,2,1,0:T(8,128)S(1)}, f32[2,16,8,256]{3,2,1,0:T(8,128)}, u32[]{:S(2)}) %copy-start.2) | copy-done | bytes 262168
  62.4 0.0 copy-start.3
  62.4 0.9 %copy-done.3 = bf16[512,256]{1,0:T(8,128)(2,1)S(1)} copy-done((bf16[512,256]{1,0:T(8,128)(2,1)S(1)}, bf16[512,256]{1,0:T(8,128)(2,1)}, u32[]{:S(2)}) %copy-start.3) | copy-done | bytes 262168
  63.4 10.6 %shard_map.105 = (f32[2,16,16,2048]{3,2,1,0:T(8,128)}, f32[2,16,8,256]{3,2,1,0:T(8,128)}) custom-call(bf16[256,128,128]{2,1,0:T(8,128)(2,1)S(1)} %copy-done, f32[2,16,16,2048]{3,2,1,0:T(8,128)S(1)} %copy-done.1, f32[2,16,8,256]{3,2,1,0:T(8,128)S(1)} %copy-done.2, bf16[512,256]{1,0:T(8,128)(2,1)S(1)} %copy-done.3, s32[1,256]{1,0:T(1,128)S(1)} %bitcast.4, ...), custom_call_target="tpu_custom_call" | custom-call | flops 2000000000 | bytes 17000000 | tf_op jit(solution)/shard_map/pallas_call | solution.py:608
Async XLA Ops:
  1.3 54.6 %copy-start.4 = (s32[256,1]{0,1:T(1,128)S(1)}, s32[256,1]{0,1:T(1,128)}, u32[]{:S(2)}) copy-start(s32[256,1]{0,1:T(1,128)} %param.14) | copy-start | bytes 3076
  1.3 54.6 %copy-start.5 = (s32[256]{0:T(256)S(1)}, s32[256]{0:T(256)}, u32[]{:S(2)}) copy-start(s32[256]{0:T(256)} %param.15) | copy-start | bytes 3076
  1.3 54.6 %copy-start.6 = (s32[256]{0:T(256)S(1)}, s32[256]{0:T(256)}, u32[]{:S(2)}) copy-start(s32[256]{0:T(256)} %param.16) | copy-start | bytes 3076
  55.9 3.4 %copy-start = (bf16[256,128,128]{2,1,0:T(8,128)(2,1)S(1)}, bf16[256,128,128]{2,1,0:T(8,128)(2,1)}, u32[]{:S(2)}) copy-start(bf16[256,128,128]{2,1,0:T(8,128)(2,1)} %w_hbm.3) | copy-start | bytes 25165828
  59.3 2.2 %copy-start.1 = (f32[2,16,16,2048]{3,2,1,0:T(8,128)S(1)}, f32[2,16,16,2048]{3,2,1,0:T(8,128)}, u32[]{:S(2)}) copy-start(f32[2,16,16,2048]{3,2,1,0:T(8,128)} %get-tuple-element.5.pre_hbm) | copy-start | bytes 12582916
  61.5 0.9 %copy-start.2 = (f32[2,16,8,256]{3,2,1,0:T(8,128)S(1)}, f32[2,16,8,256]{3,2,1,0:T(8,128)}, u32[]{:S(2)}) copy-start(f32[2,16,8,256]{3,2,1,0:T(8,128)} %get-tuple-element.6.opre_hbm) | copy-start | bytes 786436
  62.4 0.9 %copy-start.3 = (bf16[512,256]{1,0:T(8,128)(2,1)S(1)}, bf16[512,256]{1,0:T(8,128)(2,1)}, u32[]{:S(2)}) copy-start(bf16[512,256]{1,0:T(8,128)(2,1)} %get-tuple-element.7.flux_ref) | copy-start | bytes 786436

commit v3 on v2

--- a/solution.py
+++ b/solution.py
@@ -16,6 +16,14 @@
 couple = 0.5
 
 
+def over(x, n):
+    return x >> (n.bit_length() - 1)
+
+
+def within(x, n):
+    return x & (n - 1)
+
+
 def split(x):
     hi = x.astype(BF16)
     return hi, (x - hi.astype(F32)).astype(BF16)
@@ -33,13 +41,13 @@
     lev = levels.shape[0]
     size = lev * 8
     spread = (
-        lax.broadcasted_iota(I32, (size, lev), 0) // 8 == lax.broadcasted_iota(I32, (size, lev), 1)
+        over(lax.broadcasted_iota(I32, (size, lev), 0), 8) == lax.broadcasted_iota(I32, (size, lev), 1)
     ).astype(F32)
     spread_t = (
-        lax.broadcasted_iota(I32, (lev, size), 1) // 8 == lax.broadcasted_iota(I32, (lev, size), 0)
+        over(lax.broadcasted_iota(I32, (lev, size), 1), 8) == lax.broadcasted_iota(I32, (lev, size), 0)
     ).astype(F32)
     wide = exact_dot(exact_dot(spread, vertical * levels), spread_t)
-    same = lax.broadcasted_iota(I32, (size, size), 0) % 8 == lax.broadcasted_iota(I32, (size, size), 1) % 8
+    same = within(lax.broadcasted_iota(I32, (size, size), 0) ^ lax.broadcasted_iota(I32, (size, size), 1), 8) == 0
     k1 = jnp.where(same, wide, 0.0)
     k2 = exact_dot(k1, k1)
     k3 = exact_dot(k2, k1)
@@ -67,18 +75,18 @@
     for n in range(2, STEPS + 1):
         power.append(exact_dot(power[n - 1], power[1]))
     spread = (
-        lax.broadcasted_iota(I32, (size, lev), 0) // rows == lax.broadcasted_iota(I32, (size, lev), 1)
+        over(lax.broadcasted_iota(I32, (size, lev), 0), rows) == lax.broadcasted_iota(I32, (size, lev), 1)
     ).astype(F32)
     tall = [None] + [exact_dot(spread, p) for p in power[1:]]
     base = 0
     for per, first, times in ((rows, 0, 2), (8, rows, 1)):
         n_col = lev * per
         spread_c = (
-            lax.broadcasted_iota(I32, (lev, n_col), 1) // per == lax.broadcasted_iota(I32, (lev, n_col), 0)
+            over(lax.broadcasted_iota(I32, (lev, n_col), 1), per) == lax.broadcasted_iota(I32, (lev, n_col), 0)
         ).astype(F32)
         wide = [exact_dot(spread, spread_c)] + [exact_dot(p, spread_c) for p in tall[1:]]
-        x = lax.broadcasted_iota(I32, (size, n_col), 0) % rows
-        x_in = lax.broadcasted_iota(I32, (size, n_col), 1) % per + first
+        x = within(lax.broadcasted_iota(I32, (size, n_col), 0), rows)
+        x_in = within(lax.broadcasted_iota(I32, (size, n_col), 1), per) + first
         apart = jnp.abs(x_in - x)
         apart = jnp.minimum(apart, ext - apart)
         band = []
@@ -133,7 +141,7 @@
 
 
 def spread_groups(rows):
-    which = lax.broadcasted_iota(I32, rows.shape, 0) % 8
+    which = within(lax.broadcasted_iota(I32, rows.shape, 0), 8)
     return jnp.concatenate([jnp.where(which == t, rows, 0.0).astype(BF16) for t in range(8)], axis=1)
 
 
@@ -141,13 +149,17 @@
     grid_shape,
     w_hbm, atm_hbm, ocean_ref, alev_ref, olev_ref, owner_ref, block_ref, source_ref, count_ref,
     out_hbm, oout_ref, flux_ref,
-    w, atm, res, halo_src, halo_dst, halo, terms,
-    o_src, o_dst, os_src, os_dst, om_src, om_dst, oext, oterms, o_lhs, a_lhs,
-    tiles_f, contrib, acc, acc_in, send2, inbox, flux_all,
-    w_sem, atm_sem, out_sem, h_send, h_recv, o_send, o_recv, p1_sem, p2_send, p2_recv, p3_send, p3_recv, p4_sem,
+    w, atm, res, halo_src, halo_dst, halo, *more,
 ):
+    nv = atm.shape[0]
+    terms, more = more[:nv], more[nv:]
+    (
+        o_src, o_dst, os_src, os_dst, om_src, om_dst, oext, oterms, o_lhs, a_lhs,
+        tiles_f, contrib, acc, acc_in, send2, inbox, flux_all,
+        w_sem, atm_sem, out_sem, h_send, h_recv, o_send, o_recv, p1_sem, p2_send, p2_recv, p3_send, p3_recv, p4_sem,
+    ) = more
     n_grp, n_dom = grid_shape
-    nv, lev, rows, cols = atm.shape
+    _, lev, rows, cols = atm.shape
     tiles = w.shape[0]
     chunks = cols // 128
     half = n_dom // 2
@@ -211,6 +223,7 @@
     os_src[1] = edge(obottom).reshape(pairs * 8, 128).astype(BF16)
     om_src[...] = edge(ocean).reshape(nv * lev * 8, 128).astype(BF16)
 
+    strip_operator(a_lhs, alev_ref[...], rows)
     pl.semaphore_wait(barrier, 7 + nc - 1)
 
     def remote(src, dst, ssem, rsem, who):
@@ -293,7 +306,6 @@
     p1 = remote(acc.at[1 - core], acc_in, p1_sem.at[0], p1_sem.at[1], partner)
     p1.start()
     o_lhs[...] = level_terms(olev_ref[...])
-    strip_operator(a_lhs, alev_ref[...], rows)
     p1.wait_recv()
     own = acc[core] + acc_in[...]
     send2[...] = own.astype(BF16)
@@ -334,22 +346,26 @@
             oterms[:, :, t * 8:(t + 1) * 8, :] = mix(o_lhs[...], oext[:, t * 8:(t + 1) * 8, :])
         shape = (16, ocol + 128)
         r_at, c_at = lax.broadcasted_iota(I32, shape, 0), lax.broadcasted_iota(I32, shape, 1)
+        group = 8
         no_up = (r_at == 0) & (j == 0)
         no_down = (r_at == 7) & (j == n_dom - 1)
         no_left = (c_at == 0) & (g == 0)
         no_right = (c_at == ocol - 1) & (g == n_grp - 1)
 
-        def ocean_level(l, carry):
-            r = oext[l]
+        def ocean_levels(i, carry):
+            state = [oext[i * group + q] for q in range(group)]
             for k in range(STEPS):
-                total4 = jnp.where(no_up, 0.0, pltpu.roll(r, 1, 0)) + jnp.where(no_down, 0.0, pltpu.roll(r, 15, 0))
-                total4 = total4 + jnp.where(no_left, 0.0, pltpu.roll(r, 1, 1))
-                total4 = total4 + jnp.where(no_right, 0.0, pltpu.roll(r, ocol + 127, 1))
-                r = diffuse * (r + total4) + oterms[k, l]
-            oout_ref[v, l] = r[0:8, 0:ocol]
+                for q in range(group):
+                    r = state[q]
+                    near = jnp.where(no_up, 0.0, pltpu.roll(r, 1, 0)) + jnp.where(no_down, 0.0, pltpu.roll(r, 15, 0))
+                    near = near + jnp.where(no_left, 0.0, pltpu.roll(r, 1, 1))
+                    near = near + jnp.where(no_right, 0.0, pltpu.roll(r, ocol + 127, 1))
+                    state[q] = diffuse * (r + near) + oterms[k, i * group + q]
+            for q in range(group):
+                oout_ref[v, i * group + q] = state[q][0:8, 0:ocol]
             return carry
 
-        lax.fori_loop(0, lev, ocean_level, 0)
+        lax.fori_loop(0, lev // group, ocean_levels, 0)
     mine = pl.ds(pl.multiple_of(chip * obl, obl), obl)
     loop(lambda k: p2_in(k).wait_recv())
     inbox[mine, :] = send2[mine, :]
@@ -389,37 +405,45 @@
     p4 = remote(flux_all.at[core], flux_all.at[core], p4_sem.at[0], p4_sem.at[1], partner)
     p4_in = remote(flux_all.at[1 - core], flux_all.at[1 - core], p4_sem.at[0], p4_sem.at[1], partner)
 
-    for v in range(nv):
-        def unpack(i, carry):
-            at = pl.ds(pl.multiple_of((v * lev // 4 + i) * 16, 16), 16)
-            high, low = halo_dst[0, at, :].astype(F32), halo_dst[1, at, :].astype(F32)
-            for q in range(2):
-                first, second = halo_pair(high[q * 8:(q + 1) * 8], low[q * 8:(q + 1) * 8])
-                halo[4 * i + 2 * q] = first
-                halo[4 * i + 2 * q + 1] = second
-            return carry
-
-        lax.fori_loop(0, lev // 4, unpack, 0)
-
-        def along_levels(c, carry):
-            at = pl.ds(pl.multiple_of(c * width, width), width)
-            hi, lo = split(atm[v, :, :, at].reshape(lev * rows, width))
-            beyond = halo[:, :, at].reshape(lev * 8, width).astype(BF16)
-            out = dot(a_lhs[...], jnp.concatenate([hi, lo, hi, beyond, beyond], axis=0))
-            terms[:, :, :, at] = out.reshape(STEPS, lev, rows, width)
-            return carry
-
-        lax.fori_loop(0, cols // width, along_levels, 0)
-
-        def atm_level(l, carry):
+    def unpack(i, carry):
+        at = pl.ds(pl.multiple_of(i * 16, 16), 16)
+        high, low = halo_dst[0, at, :].astype(F32), halo_dst[1, at, :].astype(F32)
+        for q in range(2):
+            first, second = halo_pair(high[q * 8:(q + 1) * 8], low[q * 8:(q + 1) * 8])
+            halo[4 * i + 2 * q] = first
+            halo[4 * i + 2 * q + 1] = second
+        return carry
+
+    lax.fori_loop(0, nv * lev // 4, unpack, 0)
+    pieces = cols // width
+    group = lev // pieces
+
+    def along_levels(v, c):
+        at = pl.ds(pl.multiple_of(c * width, width), width)
+        hi, lo = split(atm[v, :, :, at].reshape(lev * rows, width))
+        beyond = halo[v * lev:(v + 1) * lev, :, at].reshape(lev * 8, width).astype(BF16)
+        out = dot(a_lhs[...], jnp.concatenate([hi, lo, hi, beyond, beyond], axis=0))
+        terms[v][:, :, :, at] = out.reshape(STEPS, lev, rows, width)
+
+    def horner(v, c):
+        for q in range(group):
+            l = c * group + q
             r = diffuse ** STEPS * atm[v, l]
             for k in range(STEPS - 1, -1, -1):
-                r = terms[k, l] + along_y(r)
+                r = terms[v][k, l] + along_y(r)
             res[v, l] = r
+
+    for v in range(nv + 1):
+        def stage(c, carry):
+            if v < nv:
+                along_levels(v, c)
+            if v > 0:
+                horner(v - 1, c)
             return carry
 
-        lax.fori_loop(0, lev, atm_level, 0)
-        out_copy(v).start()
+        lax.fori_loop(0, pieces, stage, 0)
+        if v > 0:
+            out_copy(v - 1).start()
         if v == 0:
             loop(lambda k: p3_in(k).wait_recv())
             p4.start()
@@ -480,8 +504,8 @@
     )
     hot = (lax.broadcasted_iota(I32, (tiles, 2 * span), 1) == dest_col).astype(F32).astype(BF16)
     values = dot(hot, flux_ref[...])
-    column = lax.broadcasted_iota(I32, (128, 256), 1) % 64
-    step = 4
+    column = within(lax.broadcasted_iota(I32, (128, 256), 1), 64)
+    step, sub = 16, 4
     blank = jnp.zeros((128, 128), BF16)
     for q in range(tiles // 128):
         groups = []
@@ -501,12 +525,14 @@
         acc[...] = jnp.zeros((128, 256), F32)
 
         def some(i, carry):
-            first = w[pl.ds(q * 128 + i * step, step)].reshape(step * 128, 128)
-            second = w[pl.ds(q * 128 + 64 + i * step, step)].reshape(step * 128, 128)
-            out = dot(jnp.concatenate([first, second], axis=1), rhs)
             total = acc[...]
-            for t in range(step):
-                total = jnp.where(column == i * step + t, out[t * 128:(t + 1) * 128], total)
+            for s in range(0, step, sub):
+                at = q * 128 + i * step + s
+                first = w[pl.ds(at, sub)].reshape(sub * 128, 128)
+                second = w[pl.ds(at + 64, sub)].reshape(sub * 128, 128)
+                out = dot(jnp.concatenate([first, second], axis=1), rhs)
+                for t in range(sub):
+                    total = jnp.where(column == i * step + s + t, out[t * 128:(t + 1) * 128], total)
             acc[...] = total
             return carry
 
@@ -575,8 +601,8 @@
                 pltpu.VMEM(atm_state.shape, F32),
                 pltpu.VMEM((2, pairs * 8, cols), BF16),
                 pltpu.VMEM((2, pairs * 8, cols), BF16),
-                pltpu.VMEM((lev, 8, cols), F32),
-                pltpu.VMEM((STEPS, lev, rows, cols), F32),
+                pltpu.VMEM((nv * lev, 8, cols), F32),
+                *[pltpu.VMEM((STEPS, lev, rows, cols), F32)] * nv,
                 pltpu.VMEM((2, pairs * 8, ocol), BF16),
                 pltpu.VMEM((2, pairs * 8, ocol), BF16),
                 pltpu.VMEM((2, pairs * 8, 128), BF16),
@@ -594,7 +620,7 @@
                 pltpu.VMEM((nc * obl, lanes), BF16),
                 pltpu.VMEM((nc * obl, lanes), BF16),
                 pltpu.VMEM((2, nc * obl, lanes), BF16),
-                dma((8,)), dma((nv,)), dma((nv,)),
+                dma((4,)), dma((nv,)), dma((nv,)),
                 dma((2,)), dma((2,)), dma((5,)), dma((5,)),
                 dma((2,)), dma((nc,)), dma((nc,)), dma((nc,)), dma((nc,)), dma((2,)),
             ],
@@ -622,7 +648,7 @@
                 pltpu.VMEM((rows * cols // 128, lanes), F32),
                 dma((4,)), dma((nv, 2)), dma((nv, 2)), dma((2,)),
             ],
-            compiler_params=pltpu.CompilerParams(vmem_limit_bytes=40 * 1024 * 1024),
+            compiler_params=pltpu.CompilerParams(vmem_limit_bytes=60 * 1024 * 1024),
             cost_estimate=pl.CostEstimate(flops=2_000_000_000, bytes_accessed=17_000_000, transcendentals=0),
         )(tile_weight, atm_pre, ocean_pre, flux, *tile_args)
 

time: 75.2 us -> 57.4 us (0.76); the launches traced: 73.9 us -> 57.3 us
  Pallas kernels: 65.1 us -> 56 us
  local copies, waits for them, and re-layouts: 7.48 us -> 0 us
    unnamed x14 -> x0, local copies, waits for them, and re-layouts: 7.48 us -> none
    pallas_call x1, Pallas kernels: 54.5 us -> 47.3 us  [per_device(): pl.pallas_call(functools.partial(body, (n_grp, n_dom)), out_shape=(jax.Sh...]
    pallas_call x1, Pallas kernels: 10.6 us -> 8.71 us  [per_device(): pl.pallas_call(functools.partial(back_body, obl, orow, ocol // 128), out_...]
where the time goes in v3:
time: 57.4 us; the launch traced here: 57.3 us
  Pallas kernels  56 us (98%)
  between operations  1.29 us (2%)
    pallas_call x1, Pallas kernels, per_device(): pl.pallas_call(functools.partial(body, (n_grp, n_dom)), out_shape=(jax.Sh...  47.3 us
    pallas_call x1, Pallas kernels, per_device(): pl.pallas_call(functools.partial(back_body, obl, orow, ocol // 128), out_...  8.71 us

profile of v3, /device:TPU:0, one launch (start us, length us, event | category | flops | bytes accessed | tf_op | source)
XLA Modules:
  0.0 57.3 jit_solution(8965709111946980017)
XLA Ops:
  1.3 47.3 %shard_map.104 = (f32[2,16,16,2048]{3,2,1,0:T(8,128)}, f32[2,16,8,256]{3,2,1,0:T(8,128)}, bf16[512,256]{1,0:T(8,128)(2,1)}) custom-call(bf16[256,128,128]{2,1,0:T(8,128)(2,1)} %w_hbm.3, f32[2,16,16,2048]{3,2,1,0:T(8,128)} %atm_hbm.1, f32[2,16,8,256]{3,2,1,0:T(8,128)} %ocean_ref.1, f32[16,16]{1,0:T(8,128)} %alev_ref.1, f32[16,16]{1,0:T(8,128)} %olev_ref.1, ...), custom_call_target="tpu_custom_call" | custom-call | flops 8000000000 | bytes 17000000 | tf_op jit(solution)/shard_map/pallas_call | solution.py:589
  48.5 8.7 %shard_map.105 = (f32[2,16,16,2048]{3,2,1,0:T(8,128)}, f32[2,16,8,256]{3,2,1,0:T(8,128)}) custom-call(bf16[256,128,128]{2,1,0:T(8,128)(2,1)} %w_hbm.3, f32[2,16,16,2048]{3,2,1,0:T(8,128)} %get-tuple-element.5.pre_hbm, f32[2,16,8,256]{3,2,1,0:T(8,128)} %get-tuple-element.6.opre_hbm, bf16[512,256]{1,0:T(8,128)(2,1)} %get-tuple-element.7.flux_ref, ...), custom_call_target="tpu_custom_call" | custom-call | flops 2000000000 | bytes 17000000 | tf_op jit(solution)/shard_map/pallas_call | solution.py:634

commit v4 on v3

--- a/solution.py
+++ b/solution.py
@@ -85,13 +85,13 @@
             over(lax.broadcasted_iota(I32, (lev, n_col), 1), per) == lax.broadcasted_iota(I32, (lev, n_col), 0)
         ).astype(F32)
         wide = [exact_dot(spread, spread_c)] + [exact_dot(p, spread_c) for p in tall[1:]]
-        x = within(lax.broadcasted_iota(I32, (size, n_col), 0), rows)
-        x_in = within(lax.broadcasted_iota(I32, (size, n_col), 1), per) + first
+        x = lax.broadcasted_iota(I32, (rows, 128), 0)
+        x_in = within(lax.broadcasted_iota(I32, (rows, 128), 1), per) + first
         apart = jnp.abs(x_in - x)
         apart = jnp.minimum(apart, ext - apart)
         band = []
         for m in range(STEPS + 1):
-            value = jnp.zeros((size, n_col), F32)
+            value = jnp.zeros((rows, 128), F32)
             for d in range(m + 1):
                 value = jnp.where(apart == d, diffuse ** m * BANDS[m][d], value)
             band.append(value)
@@ -99,8 +99,10 @@
             n = STEPS - k
             value = jnp.zeros((size, n_col), F32)
             for i in range(n + 1):
-                value = value + CHOOSE[n][i] * band[n - i] * wide[i]
-            hi, lo = split(CHOOSE[STEPS][k] * diffuse ** k * value)
+                part = CHOOSE[STEPS][k] * diffuse ** k * CHOOSE[n][i] * band[n - i]
+                part = jnp.concatenate([part] * (n_col // 128), axis=1)
+                value = value + jnp.concatenate([part] * lev, axis=0) * wide[i]
+            hi, lo = split(value)
             at = pl.ds(k * size, size)
             for copy in range(times):
                 out_ref[at, base + copy * n_col:base + (copy + 1) * n_col] = hi
@@ -223,7 +225,7 @@
     os_src[1] = edge(obottom).reshape(pairs * 8, 128).astype(BF16)
     om_src[...] = edge(ocean).reshape(nv * lev * 8, 128).astype(BF16)
 
-    strip_operator(a_lhs, alev_ref[...], rows)
+    o_lhs[...] = level_terms(olev_ref[...])
     pl.semaphore_wait(barrier, 7 + nc - 1)
 
     def remote(src, dst, ssem, rsem, who):
@@ -288,6 +290,43 @@
             contrib[at, 0:128] = part[0:8]
             contrib[at, 128:256] = part[8:16]
 
+    for copy in o_copies:
+        copy.wait_recv()
+    for v in range(nv):
+        m = nv * lev // 2 // nv
+        top = jnp.concatenate([o_dst[0], os_dst[0]], axis=1).astype(F32).reshape(pairs, 8, ocol + 128)
+        bottom = jnp.concatenate([o_dst[1], os_dst[1]], axis=1).astype(F32).reshape(pairs, 8, ocol + 128)
+        beside = om_dst[...].astype(F32).reshape(nv, lev, 8, 128)
+        oext[v, :, 0:8, 0:ocol] = ocean_ref[v]
+        oext[v, :, 0:8, ocol:] = beside[v]
+        for q in range(m):
+            first, second = halo_pair(top[v * m + q], bottom[v * m + q])
+            oext[v, 2 * q, 8:16, :] = first
+            oext[v, 2 * q + 1, 8:16, :] = second
+        for t in range(2):
+            oterms[v, :, :, t * 8:(t + 1) * 8, :] = mix(o_lhs[...], oext[v, :, t * 8:(t + 1) * 8, :])
+    shape = (16, ocol + 128)
+    r_at, c_at = lax.broadcasted_iota(I32, shape, 0), lax.broadcasted_iota(I32, shape, 1)
+    no_up = (r_at == 0) & (j == 0)
+    no_down = (r_at == 7) & (j == n_dom - 1)
+    no_left = (c_at == 0) & (g == 0)
+    no_right = (c_at == ocol - 1) & (g == n_grp - 1)
+    at_once = nv * lev // parts
+    per_v = lev // at_once
+
+    def ocean_levels(c):
+        v, base = c // per_v, lax.rem(c, per_v) * at_once
+        state = [oext[v, base + q] for q in range(at_once)]
+        for k in range(STEPS):
+            for q in range(at_once):
+                r = state[q]
+                near = jnp.where(no_up, 0.0, pltpu.roll(r, 1, 0)) + jnp.where(no_down, 0.0, pltpu.roll(r, 15, 0))
+                near = near + jnp.where(no_left, 0.0, pltpu.roll(r, 1, 1))
+                near = near + jnp.where(no_right, 0.0, pltpu.roll(r, ocol + 127, 1))
+                state[q] = diffuse * (r + near) + oterms[v, k, base + q]
+        for q in range(at_once):
+            oout_ref[v, base + q] = state[q][0:8, 0:ocol]
+
     def forward(c, carry):
         w_copy(c).wait()
         for s in range(per // 16):
@@ -295,6 +334,7 @@
             lhs = jnp.concatenate([spread_groups(tiles_f[2 * i]), spread_groups(tiles_f[2 * i + 1])], axis=0)
             both = w[pl.ds(i * 16, 16)].reshape(2, 1024, 128)
             keep(i, dot(lhs, jnp.concatenate([both[0], both[1]], axis=1)))
+        ocean_levels(c)
         return carry
 
     lax.fori_loop(0, parts, forward, 0)
@@ -305,7 +345,7 @@
         acc[h] = dot(hot, chi) + dot(hot, clo)
     p1 = remote(acc.at[1 - core], acc_in, p1_sem.at[0], p1_sem.at[1], partner)
     p1.start()
-    o_lhs[...] = level_terms(olev_ref[...])
+    strip_operator(a_lhs, alev_ref[...], rows)
     p1.wait_recv()
     own = acc[core] + acc_in[...]
     send2[...] = own.astype(BF16)
@@ -329,43 +369,60 @@
         lax.fori_loop(1, nc, step, 0)
 
     loop(lambda k: p2(k).start())
-    for copy in o_copies:
+    for copy in h_copies:
         copy.wait_recv()
-    for v in range(nv):
-        m = nv * lev // 2 // nv
-        top = jnp.concatenate([o_dst[0], os_dst[0]], axis=1).astype(F32).reshape(pairs, 8, ocol + 128)
-        bottom = jnp.concatenate([o_dst[1], os_dst[1]], axis=1).astype(F32).reshape(pairs, 8, ocol + 128)
-        beside = om_dst[...].astype(F32).reshape(nv, lev, 8, 128)
-        oext[:, 0:8, 0:ocol] = ocean_ref[v]
-        oext[:, 0:8, ocol:] = beside[v]
-        for q in range(m):
-            first, second = halo_pair(top[v * m + q], bottom[v * m + q])
-            oext[2 * q, 8:16, :] = first
-            oext[2 * q + 1, 8:16, :] = second
-        for t in range(2):
-            oterms[:, :, t * 8:(t + 1) * 8, :] = mix(o_lhs[...], oext[:, t * 8:(t + 1) * 8, :])
-        shape = (16, ocol + 128)
-        r_at, c_at = lax.broadcasted_iota(I32, shape, 0), lax.broadcasted_iota(I32, shape, 1)
-        group = 8
-        no_up = (r_at == 0) & (j == 0)
-        no_down = (r_at == 7) & (j == n_dom - 1)
-        no_left = (c_at == 0) & (g == 0)
-        no_right = (c_at == ocol - 1) & (g == n_grp - 1)
-
-        def ocean_levels(i, carry):
-            state = [oext[i * group + q] for q in range(group)]
-            for k in range(STEPS):
-                for q in range(group):
-                    r = state[q]
-                    near = jnp.where(no_up, 0.0, pltpu.roll(r, 1, 0)) + jnp.where(no_down, 0.0, pltpu.roll(r, 15, 0))
-                    near = near + jnp.where(no_left, 0.0, pltpu.roll(r, 1, 1))
-                    near = near + jnp.where(no_right, 0.0, pltpu.roll(r, ocol + 127, 1))
-                    state[q] = diffuse * (r + near) + oterms[k, i * group + q]
-            for q in range(group):
-                oout_ref[v, i * group + q] = state[q][0:8, 0:ocol]
+    zeros = jnp.zeros((rows, 128), F32)
+    width = 512
+
+    def out_copy(v):
+        return pltpu.make_async_copy(res.at[v], out_hbm.at[v], out_sem.at[v])
+
+    def along_y(r):
+        padded = jnp.concatenate([r, zeros], axis=1)
+        return pltpu.roll(padded, 1, 1)[:, :cols] + pltpu.roll(padded, cols + 127, 1)[:, :cols]
+
+    p4 = remote(flux_all.at[core], flux_all.at[core], p4_sem.at[0], p4_sem.at[1], partner)
+    p4_in = remote(flux_all.at[1 - core], flux_all.at[1 - core], p4_sem.at[0], p4_sem.at[1], partner)
+
+    def unpack(i, carry):
+        at = pl.ds(pl.multiple_of(i * 16, 16), 16)
+        high, low = halo_dst[0, at, :].astype(F32), halo_dst[1, at, :].astype(F32)
+        for q in range(2):
+            first, second = halo_pair(high[q * 8:(q + 1) * 8], low[q * 8:(q + 1) * 8])
+            halo[4 * i + 2 * q] = first
+            halo[4 * i + 2 * q + 1] = second
+        return carry
+
+    lax.fori_loop(0, nv * lev // 4, unpack, 0)
+    pieces = cols // width
+    group = lev // pieces
+
+    def along_levels(v, c):
+        at = pl.ds(pl.multiple_of(c * width, width), width)
+        hi, lo = split(atm[v, :, :, at].reshape(lev * rows, width))
+        beyond = halo[v * lev:(v + 1) * lev, :, at].reshape(lev * 8, width).astype(BF16)
+        out = dot(a_lhs[...], jnp.concatenate([hi, lo, hi, beyond, beyond], axis=0))
+        terms[v][:, :, :, at] = out.reshape(STEPS, lev, rows, width)
+
+    def horner(v, c):
+        for q in range(group):
+            l = c * group + q
+            r = diffuse ** STEPS * atm[v, l]
+            for k in range(STEPS - 1, -1, -1):
+                r = terms[v][k, l] + along_y(r)
+            res[v, l] = r
+
+    def stage(product, sums):
+        def one(c, carry):
+            if product is not None:
+                along_levels(product, c)
+            if sums is not None:
+                horner(sums, c)
             return carry
 
-        lax.fori_loop(0, lev // group, ocean_levels, 0)
+        lax.fori_loop(0, pieces, one, 0)
+
+    stage(0, None)
     mine = pl.ds(pl.multiple_of(chip * obl, obl), obl)
     loop(lambda k: p2_in(k).wait_recv())
     inbox[mine, :] = send2[mine, :]
@@ -390,64 +447,13 @@
         field = jnp.concatenate([flux[c * 8:(c + 1) * 8, v * 128:(v + 1) * 128] for c in range(nch)], axis=1)
         oout_ref[v, 0] = oout_ref[v, 0] + couple * field
 
-    for copy in h_copies:
-        copy.wait_recv()
-    zeros = jnp.zeros((rows, 128), F32)
-    width = 512
-
-    def out_copy(v):
-        return pltpu.make_async_copy(res.at[v], out_hbm.at[v], out_sem.at[v])
-
-    def along_y(r):
-        padded = jnp.concatenate([r, zeros], axis=1)
-        return pltpu.roll(padded, 1, 1)[:, :cols] + pltpu.roll(padded, cols + 127, 1)[:, :cols]
-
-    p4 = remote(flux_all.at[core], flux_all.at[core], p4_sem.at[0], p4_sem.at[1], partner)
-    p4_in = remote(flux_all.at[1 - core], flux_all.at[1 - core], p4_sem.at[0], p4_sem.at[1], partner)
-
-    def unpack(i, carry):
-        at = pl.ds(pl.multiple_of(i * 16, 16), 16)
-        high, low = halo_dst[0, at, :].astype(F32), halo_dst[1, at, :].astype(F32)
-        for q in range(2):
-            first, second = halo_pair(high[q * 8:(q + 1) * 8], low[q * 8:(q + 1) * 8])
-            halo[4 * i + 2 * q] = first
-            halo[4 * i + 2 * q + 1] = second
-        return carry
-
-    lax.fori_loop(0, nv * lev // 4, unpack, 0)
-    pieces = cols // width
-    group = lev // pieces
-
-    def along_levels(v, c):
-        at = pl.ds(pl.multiple_of(c * width, width), width)
-        hi, lo = split(atm[v, :, :, at].reshape(lev * rows, width))
-        beyond = halo[v * lev:(v + 1) * lev, :, at].reshape(lev * 8, width).astype(BF16)
-        out = dot(a_lhs[...], jnp.concatenate([hi, lo, hi, beyond, beyond], axis=0))
-        terms[v][:, :, :, at] = out.reshape(STEPS, lev, rows, width)
-
-    def horner(v, c):
-        for q in range(group):
-            l = c * group + q
-            r = diffuse ** STEPS * atm[v, l]
-            for k in range(STEPS - 1, -1, -1):
-                r = terms[v][k, l] + along_y(r)
-            res[v, l] = r
-
-    for v in range(nv + 1):
-        def stage(c, carry):
-            if v < nv:
-                along_levels(v, c)
-            if v > 0:
-                horner(v - 1, c)
-            return carry
-
-        lax.fori_loop(0, pieces, stage, 0)
-        if v > 0:
-            out_copy(v - 1).start()
-        if v == 0:
-            loop(lambda k: p3_in(k).wait_recv())
-            p4.start()
-
+    for v in range(1, nv):
+        stage(v, v - 1)
+        out_copy(v - 1).start()
+    loop(lambda k: p3_in(k).wait_recv())
+    p4.start()
+    stage(None, nv - 1)
+    out_copy(nv - 1).start()
     p4_in.wait_recv()
     flux_ref[...] = flux_all[...].reshape(2 * span, nv * 128)
     for copy in o_copies + h_copies + [p1, p4]:
@@ -609,8 +615,8 @@
                 pltpu.VMEM((2, pairs * 8, 128), BF16),
                 pltpu.VMEM((nv * lev * 8, 128), BF16),
                 pltpu.VMEM((nv * lev * 8, 128), BF16),
-                pltpu.VMEM((lev, 16, ocol + 128), F32),
-                pltpu.VMEM((STEPS, lev, 16, ocol + 128), F32),
+                pltpu.VMEM((nv, lev, 16, ocol + 128), F32),
+                pltpu.VMEM((nv, STEPS, lev, 16, ocol + 128), F32),
                 pltpu.VMEM((STEPS * lev * 8, 3 * lev * 8), BF16),
                 pltpu.VMEM((STEPS * lev * rows, 3 * lev * rows + 2 * lev * 8), BF16),
                 pltpu.VMEM((tiles // 8, 8 * nv, 128), F32),

time: 57.4 us -> 55.6 us (0.969)
  the two profiles are of different devices: /device:TPU:0 before, /device:TPU:1 now
where the time goes in v4:
time: 55.6 us; the launch traced here: 55.5 us
  Pallas kernels  54.2 us (97%)
  between operations  1.29 us (2%)
    pallas_call x1, Pallas kernels, per_device(): pl.pallas_call(functools.partial(body, (n_grp, n_dom)), out_shape=(jax.Sh...  45.5 us
    pallas_call x1, Pallas kernels, per_device(): pl.pallas_call(functools.partial(back_body, obl, orow, ocol // 128), out_...  8.71 us

profile of v4, /device:TPU:1, one launch (start us, length us, event | category | flops | bytes accessed | tf_op | source)
XLA Modules:
  0.0 55.5 jit_solution(12410679694676731896)
XLA Ops:
  1.3 45.5 %shard_map.104 = (f32[2,16,16,2048]{3,2,1,0:T(8,128)}, f32[2,16,8,256]{3,2,1,0:T(8,128)}, bf16[512,256]{1,0:T(8,128)(2,1)}) custom-call(bf16[256,128,128]{2,1,0:T(8,128)(2,1)} %w_hbm.3, f32[2,16,16,2048]{3,2,1,0:T(8,128)} %atm_hbm.1, f32[2,16,8,256]{3,2,1,0:T(8,128)} %ocean_ref.1, f32[16,16]{1,0:T(8,128)} %alev_ref.1, f32[16,16]{1,0:T(8,128)} %olev_ref.1, ...), custom_call_target="tpu_custom_call" | custom-call | flops 8000000000 | bytes 17000000 | tf_op jit(solution)/shard_map/pallas_call | solution.py:595
  46.7 8.7 %shard_map.105 = (f32[2,16,16,2048]{3,2,1,0:T(8,128)}, f32[2,16,8,256]{3,2,1,0:T(8,128)}) custom-call(bf16[256,128,128]{2,1,0:T(8,128)(2,1)} %w_hbm.3, f32[2,16,16,2048]{3,2,1,0:T(8,128)} %get-tuple-element.5.pre_hbm, f32[2,16,8,256]{3,2,1,0:T(8,128)} %get-tuple-element.6.opre_hbm, bf16[512,256]{1,0:T(8,128)(2,1)} %get-tuple-element.7.flux_ref, ...), custom_call_target="tpu_custom_call" | custom-call | flops 2000000000 | bytes 17000000 | tf_op jit(solution)/shard_map/pallas_call | solution.py:640

commit v5 on v4

--- a/solution.py
+++ b/solution.py
@@ -225,7 +225,18 @@
     os_src[1] = edge(obottom).reshape(pairs * 8, 128).astype(BF16)
     om_src[...] = edge(ocean).reshape(nv * lev * 8, 128).astype(BF16)
 
-    o_lhs[...] = level_terms(olev_ref[...])
+    for v in range(nv):
+        atm_copy(v).wait()
+    def pack_halo(i, carry):
+        v, pair = i // (lev // 4), lax.rem(i, lev // 4) * 4
+        top, _ = pack_pairs(atm[v, pl.ds(pair, 4), 0:8, :])
+        _, bottom = pack_pairs(atm[v, pl.ds(pair, 4), rows - 8:rows, :])
+        span = pl.ds(pl.multiple_of(i * 16, 16), 16)
+        halo_src[0, span, :] = top.reshape(16, cols).astype(BF16)
+        halo_src[1, span, :] = bottom.reshape(16, cols).astype(BF16)
+        return carry
+
+    lax.fori_loop(0, nv * lev // 4, pack_halo, 0)
     pl.semaphore_wait(barrier, 7 + nc - 1)
 
     def remote(src, dst, ssem, rsem, who):
@@ -243,25 +254,18 @@
     for copy in o_copies:
         copy.start()
 
-    for v in range(nv):
-        atm_copy(v).wait()
-    h_copies = [
-        remote(halo_src.at[0], halo_dst.at[0], h_send.at[0], h_recv.at[0], left),
-        remote(halo_src.at[1], halo_dst.at[1], h_send.at[1], h_recv.at[1], right),
-    ]
-
-    def pack_halo(i, carry):
-        v, pair = i // (lev // 4), lax.rem(i, lev // 4) * 4
-        top, _ = pack_pairs(atm[v, pl.ds(pair, 4), 0:8, :])
-        _, bottom = pack_pairs(atm[v, pl.ds(pair, 4), rows - 8:rows, :])
-        span = pl.ds(pl.multiple_of(i * 16, 16), 16)
-        halo_src[0, span, :] = top.reshape(16, cols).astype(BF16)
-        halo_src[1, span, :] = bottom.reshape(16, cols).astype(BF16)
-        return carry
-
-    lax.fori_loop(0, nv * lev // 4, pack_halo, 0)
+    share = pairs * 8 // nv
+    h_copies = []
+    for v in range(nv):
+        at = pl.ds(v * share, share)
+        for side_at, who in ((0, left), (1, right)):
+            sem = v * 2 + side_at
+            h_copies.append(
+                remote(halo_src.at[side_at, at], halo_dst.at[side_at, at], h_send.at[sem], h_recv.at[sem], who)
+            )
     for copy in h_copies:
         copy.start()
+    o_lhs[...] = level_terms(olev_ref[...])
 
     nch = ocol // 128
     span = nc * obl
@@ -369,8 +373,6 @@
         lax.fori_loop(1, nc, step, 0)
 
     loop(lambda k: p2(k).start())
-    for copy in h_copies:
-        copy.wait_recv()
     zeros = jnp.zeros((rows, 128), F32)
     width = 512
 
@@ -393,7 +395,11 @@
             halo[4 * i + 2 * q + 1] = second
         return carry
 
-    lax.fori_loop(0, nv * lev // 4, unpack, 0)
+    def halo_in(v):
+        for copy in h_copies[2 * v:2 * v + 2]:
+            copy.wait_recv()
+        lax.fori_loop(v * lev // 4, (v + 1) * lev // 4, unpack, 0)
+
     pieces = cols // width
     group = lev // pieces
 
@@ -422,6 +428,7 @@
 
         lax.fori_loop(0, pieces, one, 0)
 
+    halo_in(0)
     stage(0, None)
     mine = pl.ds(pl.multiple_of(chip * obl, obl), obl)
     loop(lambda k: p2_in(k).wait_recv())
@@ -448,6 +455,7 @@
         oout_ref[v, 0] = oout_ref[v, 0] + couple * field
 
     for v in range(1, nv):
+        halo_in(v)
         stage(v, v - 1)
         out_copy(v - 1).start()
     loop(lambda k: p3_in(k).wait_recv())
@@ -627,7 +635,7 @@
                 pltpu.VMEM((nc * obl, lanes), BF16),
                 pltpu.VMEM((2, nc * obl, lanes), BF16),
                 dma((4,)), dma((nv,)), dma((nv,)),
-                dma((2,)), dma((2,)), dma((5,)), dma((5,)),
+                dma((2 * nv,)), dma((2 * nv,)), dma((5,)), dma((5,)),
                 dma((2,)), dma((nc,)), dma((nc,)), dma((nc,)), dma((nc,)), dma((2,)),
             ],
             compiler_params=pltpu.CompilerParams(

time: 55.6 us -> 57.3 us (1.031)
  the two profiles are of different devices: /device:TPU:1 before, /device:TPU:0 now
where the time goes in v5:
time: 57.3 us; the launch traced here: 57.1 us
  Pallas kernels  55.8 us (97%)
  between operations  1.29 us (2%)
    pallas_call x1, Pallas kernels, per_device(): pl.pallas_call(functools.partial(body, (n_grp, n_dom)), out_shape=(jax.Sh...  47.1 us
    pallas_call x1, Pallas kernels, per_device(): pl.pallas_call(functools.partial(back_body, obl, orow, ocol // 128), out_...  8.71 us

profile of v5, /device:TPU:0, one launch (start us, length us, event | category | flops | bytes accessed | tf_op | source)
XLA Modules:
  0.0 57.1 jit_solution(10936999310385083720)
XLA Ops:
  1.3 47.1 %shard_map.104 = (f32[2,16,16,2048]{3,2,1,0:T(8,128)}, f32[2,16,8,256]{3,2,1,0:T(8,128)}, bf16[512,256]{1,0:T(8,128)(2,1)}) custom-call(bf16[256,128,128]{2,1,0:T(8,128)(2,1)} %w_hbm.3, f32[2,16,16,2048]{3,2,1,0:T(8,128)} %atm_hbm.1, f32[2,16,8,256]{3,2,1,0:T(8,128)} %ocean_ref.1, f32[16,16]{1,0:T(8,128)} %alev_ref.1, f32[16,16]{1,0:T(8,128)} %olev_ref.1, ...), custom_call_target="tpu_custom_call" | custom-call | flops 8000000000 | bytes 17000000 | tf_op jit(solution)/shard_map/pallas_call | solution.py:603
  48.4 8.7 %shard_map.105 = (f32[2,16,16,2048]{3,2,1,0:T(8,128)}, f32[2,16,8,256]{3,2,1,0:T(8,128)}) custom-call(bf16[256,128,128]{2,1,0:T(8,128)(2,1)} %w_hbm.3, f32[2,16,16,2048]{3,2,1,0:T(8,128)} %get-tuple-element.5.pre_hbm, f32[2,16,8,256]{3,2,1,0:T(8,128)} %get-tuple-element.6.opre_hbm, bf16[512,256]{1,0:T(8,128)(2,1)} %get-tuple-element.7.flux_ref, ...), custom_call_target="tpu_custom_call" | custom-call | flops 2000000000 | bytes 17000000 | tf_op jit(solution)/shard_map/pallas_call | solution.py:648

commit v6 on v4

--- a/solution.py
+++ b/solution.py
@@ -35,6 +35,20 @@
 
 def exact_dot(a, b):
     return jnp.dot(a, b, preferred_element_type=F32, precision=lax.Precision.HIGHEST)
+
+
+def thirds(x):
+    hi, rest = x.astype(BF16), x - x.astype(BF16).astype(F32)
+    mid = rest.astype(BF16)
+    return [hi, mid, (rest - mid.astype(F32)).astype(BF16)]
+
+
+def spread_rows(ones, x):
+    return dot(jnp.concatenate([ones.astype(BF16)] * 3, axis=1), jnp.concatenate(thirds(x), axis=0))
+
+
+def spread_columns(x, ones):
+    return dot(jnp.concatenate(thirds(x), axis=1), jnp.concatenate([ones.astype(BF16)] * 3, axis=0))
 
 
 def level_terms(levels):
@@ -46,7 +60,7 @@
     spread_t = (
         over(lax.broadcasted_iota(I32, (lev, size), 1), 8) == lax.broadcasted_iota(I32, (lev, size), 0)
     ).astype(F32)
-    wide = exact_dot(exact_dot(spread, vertical * levels), spread_t)
+    wide = spread_columns(spread_rows(spread, vertical * levels), spread_t)
     same = within(lax.broadcasted_iota(I32, (size, size), 0) ^ lax.broadcasted_iota(I32, (size, size), 1), 8) == 0
     k1 = jnp.where(same, wide, 0.0)
     k2 = exact_dot(k1, k1)
@@ -77,14 +91,14 @@
     spread = (
         over(lax.broadcasted_iota(I32, (size, lev), 0), rows) == lax.broadcasted_iota(I32, (size, lev), 1)
     ).astype(F32)
-    tall = [None] + [exact_dot(spread, p) for p in power[1:]]
+    tall = [None] + [spread_rows(spread, p) for p in power[1:]]
     base = 0
     for per, first, times in ((rows, 0, 2), (8, rows, 1)):
         n_col = lev * per
         spread_c = (
             over(lax.broadcasted_iota(I32, (lev, n_col), 1), per) == lax.broadcasted_iota(I32, (lev, n_col), 0)
         ).astype(F32)
-        wide = [exact_dot(spread, spread_c)] + [exact_dot(p, spread_c) for p in tall[1:]]
+        wide = [dot(spread.astype(BF16), spread_c.astype(BF16))] + [spread_columns(p, spread_c) for p in tall[1:]]
         x = lax.broadcasted_iota(I32, (rows, 128), 0)
         x_in = within(lax.broadcasted_iota(I32, (rows, 128), 1), per) + first
         apart = jnp.abs(x_in - x)

time: 55.6 us -> 55.6 us (level)
  no operation moved by 1% of the time
where the time goes in v6:
time: 55.6 us; the launch traced here: 55.4 us
  Pallas kernels  54.2 us (97%)
  between operations  1.29 us (2%)
    pallas_call x1, Pallas kernels, per_device(): pl.pallas_call(functools.partial(body, (n_grp, n_dom)), out_shape=(jax.Sh...  45.5 us
    pallas_call x1, Pallas kernels, per_device(): pl.pallas_call(functools.partial(back_body, obl, orow, ocol // 128), out_...  8.71 us

profile of v6, /device:TPU:1, one launch (start us, length us, event | category | flops | bytes accessed | tf_op | source)
XLA Modules:
  0.0 55.4 jit_solution(13918675718969910451)
XLA Ops:
  1.3 45.5 %shard_map.104 = (f32[2,16,16,2048]{3,2,1,0:T(8,128)}, f32[2,16,8,256]{3,2,1,0:T(8,128)}, bf16[512,256]{1,0:T(8,128)(2,1)}) custom-call(bf16[256,128,128]{2,1,0:T(8,128)(2,1)} %w_hbm.3, f32[2,16,16,2048]{3,2,1,0:T(8,128)} %atm_hbm.1, f32[2,16,8,256]{3,2,1,0:T(8,128)} %ocean_ref.1, f32[16,16]{1,0:T(8,128)} %alev_ref.1, f32[16,16]{1,0:T(8,128)} %olev_ref.1, ...), custom_call_target="tpu_custom_call" | custom-call | flops 8000000000 | bytes 17000000 | tf_op jit(solution)/shard_map/pallas_call | solution.py:609
  46.7 8.7 %shard_map.105 = (f32[2,16,16,2048]{3,2,1,0:T(8,128)}, f32[2,16,8,256]{3,2,1,0:T(8,128)}) custom-call(bf16[256,128,128]{2,1,0:T(8,128)(2,1)} %w_hbm.3, f32[2,16,16,2048]{3,2,1,0:T(8,128)} %get-tuple-element.5.pre_hbm, f32[2,16,8,256]{3,2,1,0:T(8,128)} %get-tuple-element.6.opre_hbm, bf16[512,256]{1,0:T(8,128)(2,1)} %get-tuple-element.7.flux_ref, ...), custom_call_target="tpu_custom_call" | custom-call | flops 2000000000 | bytes 17000000 | tf_op jit(solution)/shard_map/pallas_call | solution.py:654
